TPU v7x, 128 devices: a whole 4x4x4 slice. The times are simulated.
128 devices in a mesh: dp: 4 (over y_lo, core), ep: 32 (over x, y_hi, z).
Axes of the slice: x: 4, y: 4 (y_hi: 2, y_lo: 2; y = y_hi * 2 + y_lo), z: 4, core: 2. Of those that a mesh axis runs over, the one named last changes fastest.
Arguments:
- latent_pool: bfloat16 [16384, 36864], P(('dp', 'ep')), may hold values from -6 to 6
- queries: bfloat16 [2048, 73728], P(('dp', 'ep')), may hold values from -72 to 72, as said below
- hidden: bfloat16 [2048, 7168], P(('dp', 'ep')), may hold values from -6 to 6
- lengths: int32 [128, 16], P(('dp', 'ep')), may hold values from 1 to 512, 5120 in all within a row
- page_table: int32 [128, 128], P(('dp', 'ep')), may hold values from 0 to 127, each once within a row
- send_slot: int32 [128, 2], P(('dp', 'ep')), may hold values from 0 to 15, as said below
- match: int32 [32, 2], P('ep'), may hold values from 1 to 3
- routes: int32 [2048, 8], P(('dp', 'ep')), may hold values from 0 to 31, all different within a row; in each aligned block of 16 rows (0 to 15, 16 to 31, ...) at most 8 rows name the same one
- route_gain: int32 [2048, 8], P(('dp', 'ep')), may hold values from 1 to 16
- w_gate: bfloat16 [32, 7168, 1024], P('ep', None, 'dp'), may hold values from -0.0625 to 0.0625
- w_up: bfloat16 [32, 7168, 1024], P('ep', None, 'dp'), may hold values from -0.0625 to 0.0625
- w_down: bfloat16 [32, 1024, 7168], P('ep', 'dp'), may hold values from -0.1875 to 0.1875
Outputs:
- attn_context: bfloat16 [2048, 65536], P(('dp', 'ep'))
- moe_out: bfloat16 [2048, 7168], P(('dp', 'ep'))
Inputs may be any that keep to these rules, and one draw needn't show every extreme that they name: queries are finite. `send_slot`: the 2 slots listed for one device are different. `match`: a swap's partner replica is the replica index xor this value; it is the same for all replicas of one ep index. `routes`: each row names 8 different experts; among the 16 rows of one device no expert is named by more than 8 rows, a bound that some block reaches. `page_table`: the slot s request's pages are entries s * 8 to s * 8 + 7 of its device's row, in logical order; each row is a permutation.
All inputs are finite; a program needn't handle non-finite values.
Results may differ from a plain program's by a relative error of at most 0.015.
Values may be sent and summed in bfloat16 or wider, within the bound.
No kernel may reach another device: no remote copies, remote signals or barrier semaphores. Data moves between devices by JAX's collectives and lax.ppermute only.
A program may use at most 192 MiB of HBM per device.

v0:
```python
import jax
import jax.numpy as jnp
from jax import lax
from jax.sharding import Mesh, PartitionSpec as P

HEADS = 128
ROPE = 64
TOP = 8

score_scale = 192.0 ** (-0.5)
gain_step = 0.0625

ALL = ("yl", "core", "x", "yh", "z")
PEERS = ("yl", "x", "yh", "z")


def flip(value, axes, mask):
    return lax.ppermute(value, axes, [(i, i ^ mask) for i in range(4 if len(axes) == 2 else 2)])


def swapped(rows, flips):
    by_one = flip(rows, ("core",), 1)
    by_two = flip(rows, ("yl",), 1)
    by_three = flip(rows, ("yl", "core"), 3)
    which = flips.reshape((-1,) + (1,) * (rows.ndim - 1))
    return jnp.where(which == 1, by_one, jnp.where(which == 2, by_two, by_three))


def attend(latent_pool, queries, lengths, page_table):
    row_count = queries.shape[0]
    kv_width = queries.shape[1] // HEADS
    latent_width = kv_width - ROPE
    pages = latent_pool.reshape(latent_pool.shape[0], -1, kv_width)
    key_cache = pages[page_table.reshape(-1)].reshape(row_count, -1, kv_width)
    key_span = key_cache.shape[1]
    positions = lax.broadcasted_iota(jnp.int32, (row_count, key_span), 1)
    key_valid = positions < lengths.reshape(row_count, 1)
    query_heads = queries.reshape(row_count, HEADS, kv_width)
    scores = (
        jnp.einsum("rhc,rtc->rht", query_heads, key_cache, preferred_element_type=jnp.float32)
        * score_scale
    )
    scores = jnp.where(key_valid[:, None, :], scores, -1e30)
    row_max = jnp.max(scores, axis=2, keepdims=True)
    weights = jnp.exp(scores - row_max)
    weights = weights / jnp.sum(weights, axis=2, keepdims=True)
    context = jnp.einsum(
        "rht,rtc->rhc",
        weights.astype(jnp.bfloat16),
        key_cache[:, :, :latent_width],
        preferred_element_type=jnp.float32,
    )
    return context.astype(jnp.bfloat16).reshape(row_count, HEADS * latent_width)


def body(
    latent_pool,
    queries,
    hidden,
    lengths,
    page_table,
    send_slot,
    match,
    routes,
    route_gain,
    w_gate,
    w_up,
    w_down,
):
    experts = 32
    row_count = queries.shape[0]
    model_width = hidden.shape[1]
    out_slots = send_slot.reshape(-1)
    flips = match.reshape(-1)

    arriving = swapped(hidden[out_slots], flips)
    slots = jnp.arange(row_count, dtype=jnp.int32)
    leaving = (slots[:, None] == out_slots[None, :]).astype(jnp.float32)
    staying = 1.0 - jnp.sum(leaving, axis=1)

    capacity = min(row_count, max(2, 2 * row_count * TOP // experts))
    expert_ids = jnp.arange(experts, dtype=jnp.int32)
    named = (routes[:, :, None] == expert_ids).astype(jnp.int32)
    chosen = jnp.sum(named, axis=1)
    rank = jnp.cumsum(chosen, axis=0) - chosen
    gain_of = jnp.sum(named * route_gain[:, :, None], axis=1).astype(jnp.float32) * gain_step
    at_slot = (rank[:, :, None] == jnp.arange(capacity, dtype=jnp.int32)) & (chosen[:, :, None] > 0)
    table = at_slot.astype(jnp.float32).reshape(row_count, experts * capacity)
    gain_table = jnp.where(at_slot, gain_of[:, :, None], 0.0).reshape(row_count, experts * capacity)

    picks = jnp.concatenate([table * staying[:, None], jnp.dot(leaving.T, table)], axis=0)
    picks = jnp.concatenate([picks, picks], axis=1).astype(jnp.bfloat16)
    rows = jnp.concatenate([hidden, arriving], axis=0)
    outgoing = lax.dot_general(
        picks, rows, (((0,), (0,)), ((), ())), preferred_element_type=jnp.float32
    )
    outgoing = outgoing.astype(jnp.bfloat16).reshape(2 * experts, capacity, model_width)
    arrived = lax.all_to_all(outgoing, PEERS, split_axis=0, concat_axis=0, tiled=True)
    arrived = arrived.reshape(2 * experts * capacity, model_width)

    gate_other = flip(w_gate[0], ("core",), 1)
    up_other = flip(w_up[0], ("core",), 1)
    down_other = flip(w_down[0], ("core",), 1)

    context = attend(latent_pool, queries, lengths, page_table)

    def units(gate, up):
        gate_proj = jnp.dot(arrived, gate, preferred_element_type=jnp.float32)
        up_proj = jnp.dot(arrived, up, preferred_element_type=jnp.float32)
        return (jax.nn.silu(gate_proj) * up_proj).astype(jnp.bfloat16)

    activated = jnp.concatenate([units(w_gate[0], w_up[0]), units(gate_other, up_other)], axis=1)
    down = jnp.concatenate([w_down[0], down_other], axis=0)
    partial = jnp.dot(activated, down, preferred_element_type=jnp.float32).astype(jnp.bfloat16)
    returned = lax.all_to_all(
        partial.reshape(2 * experts, capacity, model_width),
        PEERS,
        split_axis=0,
        concat_axis=0,
        tiled=True,
    ).reshape(2 * experts * capacity, model_width)
    mix = jnp.concatenate([gain_table, gain_table], axis=1).astype(jnp.bfloat16)
    moe_out = jnp.dot(mix, returned, preferred_element_type=jnp.float32).astype(jnp.bfloat16)

    back = swapped(context[out_slots], flips)
    for k in range(out_slots.shape[0]):
        context = lax.dynamic_update_slice_in_dim(context, back[k : k + 1], out_slots[k], 0)
    return (context, moe_out)


def solution(mesh):
    fine = Mesh(mesh.devices.reshape(2, 2, 4, 2, 4), ALL)
    rows = P(ALL, None)
    column = ("x", "yh", "z")
    replica = ("yl", "core")
    placed = (
        rows,
        rows,
        rows,
        rows,
        rows,
        rows,
        P(column, None),
        rows,
        rows,
        P(column, None, replica),
        P(column, None, replica),
        P(column, replica, None),
    )
    return jax.shard_map(body, mesh=fine, in_specs=placed, out_specs=(rows, rows), check_vma=False)
```

profile of v0, /device:TPU:58, one launch (start us, length us, event | category | flops | bytes accessed | tf_op | source)
XLA Modules:
  0.0 353.0 jit_solution(2834469471059580286)
XLA Ops:
  0.6 0.7 fusion.48
  1.3 2.2 gather_fusion.2
  3.5 0.0 collective-permute-start.3
  3.5 0.7 collective-permute-start.4
  4.2 1.1 collective-permute-start.5
  5.3 12.6 %copy.63 = bf16[128,36864]{0,1:T(8,128)(2,1)} copy(bf16[128,36864]{1,0:T(8,128)(2,1)} %param.12) | data formatting | bytes 18874368 | tf_op args[0]
  18.0 14.8 %copy.64 = bf16[128,64,576]{2,1,0:T(8,128)(2,1)} copy(bf16[128,64,576]{0,2,1:T(8,128)(2,1)} %bitcast.73) | data formatting | bytes 18874368 | tf_op jit(solution)/shard_map/reshape | solution.py:33
  32.8 4.4 %reshape.170 = bf16[16,128,576]{2,1,0:T(8,128)(2,1)S(1)} reshape(bf16[16,73728]{1,0:T(8,128)(2,1)} %param.13) | data formatting | bytes 4718592 | tf_op jit(solution)/shard_map/reshape | solution.py:38
  37.2 0.1 iota_compare_fusion.1
  37.3 11.7 %gather_fusion = bf16[128,64,576]{2,1,0:T(8,128)(2,1)} fusion(bf16[128,64,576]{2,1,0:T(8,128)(2,1)} %copy.64, s32[1024]{0:T(1024)S(1)} %pad_clamp_fusion.1), kind=kCustom, calls=%fused_computation | custom fusion | bytes 18874880 | tf_op jit(solution)/shard_map/gather | solution.py:34
  49.0 7.4 %fusion.59 = (f32[16,128]{1,0:T(8,128)S(1)}, f32[16,128,512]{1,2,0:T(8,128)}) fusion(pred[16,512]{1,0:T(8,128)(4,1)S(1)} %iota_compare_fusion.1, bf16[16,512,576]{2,1,0:T(8,128)(2,1)} %bitcast.74, bf16[16,128,576]{2,1,0:T(8,128)(2,1)S(1)} %reshape.170), kind=kOutput, calls=%fused_computation.88 | convolution fusion | flops 1212154368 | bytes 16007168 | tf_op jit(solution)/shard_map/sub | solution.py:45
  56.4 6.1 %fusion.25 = bf16[16,128,512]{2,1,0:T(8,128)(2,1)S(1)} fusion(bf16[16,512,576]{2,1,0:T(8,128)(2,1)} %bitcast.75, f32[16,128,512]{1,2,0:T(8,128)} %get-tuple-element.13, f32[16,128]{1,0:T(8,128)S(1)} %get-tuple-element.12), kind=kOutput, calls=%fused_computation.33 | convolution fusion | flops 1076887552 | bytes 14688256 | tf_op jit(solution)/shard_map/rht,rtc->rhc/dot_general | solution.py:47
  62.5 0.0 copy-start.2
  62.5 0.0 copy-start.3
  62.5 0.0 copy-start.4
  62.5 0.0 copy-start.9
  62.5 0.0 copy-start.1
  62.6 1.2 copy.79
  63.7 0.9 gather_fusion.1
  64.6 0.4 collective-permute-start
  65.0 0.7 collective-permute-start.1
  65.7 0.1 copy.68
  65.8 0.1 copy.73
  65.9 0.1 select_reduce_fusion
  66.0 0.1 copy.69
  66.1 0.1 copy.70
  66.2 0.1 copy.71
  66.3 0.1 copy.72
  66.4 0.1 copy.74
  66.5 0.1 copy.75
  66.6 0.1 eq.84
  66.7 0.1 convert_reduce_fusion.1
  66.8 0.2 fusion.46
  67.0 0.1 broadcast_select_fusion.4
  67.1 0.6 fusion.58
  71.5 0.0 collective-permute-done.3
  71.5 0.9 collective-permute-start.2
  72.4 0.0 collective-permute-done.4
  72.4 0.6 collective-permute-start.6
  73.0 0.3 collective-permute-start.7
  73.3 0.9 broadcast_select_fusion.3
  74.2 5.1 %fusion.1 = bf16[64,8,7168]{2,1,0:T(8,128)(2,1)} fusion(bf16[2,7168]{1,0:T(2,128)(2,1)S(1)} %broadcast_select_fusion.3, bf16[16,7168]{1,0:T(8,128)(2,1)S(1)} %copy-done.1, bf16[18,256]{1,0:T(8,128)(2,1)S(1)} %maximum_convert_fusion), kind=kOutput, calls=%fused_computation.6 | convolution fusion | flops 136343552 | bytes 7607296 | tf_op jit(solution)/shard_map/dot_general | solution.py:94
  79.3 11.1 %all-to-all-start = ((bf16[64,8,7168]{2,1,0:T(8,128)(2,1)}), bf16[64,8,7168]{2,1,0:T(8,128)(2,1)}, u32[]{:S(2)}, u32[]{:S(2)}) async-start(bf16[64,8,7168]{2,1,0:T(8,128)(2,1)} %fusion.1), calls=%async_computation | async-start | bytes 14680064 | tf_op jit(solution)/shard_map/all_to_all | solution.py:98
  90.3 0.0 collective-permute-done
  90.4 0.1 collective-permute-start.8
  90.4 0.0 collective-permute-done.1
  90.5 0.0 collective-permute-done.2
  90.5 0.5 broadcast_select_fusion.1
  90.9 109.3 %all-to-all-done = bf16[64,8,7168]{2,1,0:T(8,128)(2,1)} async-done(((bf16[64,8,7168]{2,1,0:T(8,128)(2,1)}), bf16[64,8,7168]{2,1,0:T(8,128)(2,1)}, u32[]{:S(2)}, u32[]{:S(2)}) %all-to-all-start) | async-done | bytes 7340064 | tf_op jit(solution)/shard_map/all_to_all | solution.py:98
  200.2 6.2 %fusion.15 = f32[512,256]{0,1:T(8,128)S(1)} fusion(bf16[64,8,7168]{2,1,0:T(8,128)(2,1)} %all-to-all-done, bf16[1,7168,256]{2,1,0:T(8,128)(2,1)} %param.21), kind=kOutput, calls=%fused_computation.21 | convolution fusion | flops 1879048192 | bytes 11534336 | tf_op jit(solution)/shard_map/dot_general | solution.py:108
  206.4 0.0 copy-start.6
  206.5 6.4 %fusion.11 = f32[512,256]{0,1:T(8,128)S(1)} fusion(bf16[7168,256]{1,0:T(8,128)(2,1)} %collective-permute-done.6, bf16[64,8,7168]{2,1,0:T(8,128)(2,1)} %all-to-all-done), kind=kOutput, calls=%fused_computation.17 | convolution fusion | flops 1879048192 | bytes 11534336 | tf_op jit(solution)/shard_map/dot_general | solution.py:108
  212.9 5.2 %fusion.31 = bf16[512,256]{0,1:T(8,128)(2,1)S(1)} fusion(bf16[64,8,7168]{2,1,0:T(8,128)(2,1)} %all-to-all-done, f32[512,256]{0,1:T(8,128)S(1)} %fusion.15, bf16[1,7168,256]{2,1,0:T(8,128)(2,1)S(1)} %copy-done.6), kind=kOutput, calls=%fused_computation.35 | convolution fusion | flops 1879834624 | bytes 11796480 | tf_op jit(solution)/shard_map/dot_general | solution.py:109
  218.1 0.0 copy-start.7
  218.1 0.0 collective-permute-done.7
  218.1 6.4 %multiply_convert_fusion = bf16[512,256]{0,1:T(8,128)(2,1)S(1)} fusion(f32[512,256]{0,1:T(8,128)S(1)} %fusion.11, bf16[7168,256]{1,0:T(8,128)(2,1)} %collective-permute-done.7, bf16[64,8,7168]{2,1,0:T(8,128)(2,1)} %all-to-all-done), kind=kOutput, calls=%fused_computation.39 | convolution fusion | flops 1879834624 | bytes 11796480 | tf_op jit(solution)/shard_map/dot_general | solution.py:109
  224.5 9.3 %fusion.2 = bf16[64,8,7168]{2,1,0:T(8,128)(2,1)} fusion(bf16[256,7168]{1,0:T(8,128)(2,1)} %collective-permute-done.8, bf16[256,7168]{1,0:T(8,128)(2,1)S(1)} %bitcast.85, bf16[512,256]{0,1:T(8,128)(2,1)S(1)} %multiply_convert_fusion, bf16[512,256]{0,1:T(8,128)(2,1)S(1)} %fusion.31), kind=kOutput, calls=%fused_computation.7 | convolution fusion | flops 3777495040 | bytes 15204352 | tf_op jit(solution)/shard_map/dot_general | solution.py:114
  233.8 8.3 %all-to-all-start.1 = ((bf16[64,8,7168]{2,1,0:T(8,128)(2,1)}), bf16[64,8,7168]{2,1,0:T(8,128)(2,1)}, u32[]{:S(2)}, u32[]{:S(2)}) async-start(bf16[64,8,7168]{2,1,0:T(8,128)(2,1)} %fusion.2), calls=%async_computation.1 | async-start | bytes 14680064 | tf_op jit(solution)/shard_map/all_to_all | solution.py:115
  242.1 0.4 fusion.57
  242.4 4.4 %dynamic_update_slice.6 = bf16[16,65536]{1,0:T(8,128)(2,1)S(1)} dynamic-update-slice(bf16[16,65536]{1,0:T(8,128)(2,1)S(1)} %bitcast.77, bf16[1,65536]{1,0:T(2,128)(2,1)S(1)} %get-tuple-element.7, s32[]{:T(128)S(6)} %select_n.59, s32[]{:T(128)} %constant.11.clone.1) | dynamic-update-slice | bytes 262148 | tf_op jit(solution)/shard_map/dynamic_update_slice | solution.py:127
  246.9 4.4 %dynamic_update_slice.7 = bf16[16,65536]{1,0:T(8,128)(2,1)S(1)} dynamic-update-slice(bf16[16,65536]{1,0:T(8,128)(2,1)S(1)} %dynamic_update_slice.6, bf16[1,65536]{1,0:T(2,128)(2,1)S(1)} %get-tuple-element.6, s32[]{:T(128)S(6)} %select_n.60, s32[]{:T(128)} %constant.11.clone.1) | dynamic-update-slice | bytes 262148 | tf_op jit(solution)/shard_map/dynamic_update_slice | solution.py:127
  251.3 0.0 copy-start
  251.3 96.8 %all-to-all-done.1 = bf16[64,8,7168]{2,1,0:T(8,128)(2,1)} async-done(((bf16[64,8,7168]{2,1,0:T(8,128)(2,1)}), bf16[64,8,7168]{2,1,0:T(8,128)(2,1)}, u32[]{:S(2)}, u32[]{:S(2)}) %all-to-all-start.1) | async-done | bytes 7340064 | tf_op jit(solution)/shard_map/all_to_all | solution.py:115
  348.1 4.8 %convolution_convert_fusion.2 = bf16[16,7168]{1,0:T(8,128)(2,1)} fusion(bf16[64,8,7168]{2,1,0:T(8,128)(2,1)} %all-to-all-done.1, bf16[16,256]{1,0:T(8,128)(2,1)S(1)} %get-tuple-element.4), kind=kOutput, calls=%fused_computation.10 | convolution fusion | flops 117587968 | bytes 7577600 | tf_op jit(solution)/shard_map/dot_general | solution.py:123
  (30 shorter events, 0.2 us)
Async XLA Ops:
  3.5 68.0 %collective-permute-start.3 = (bf16[2,7168]{1,0:T(2,128)(2,1)}, bf16[2,7168]{1,0:T(2,128)(2,1)S(1)}, u32[]{:S(2)}, u32[]{:S(2)}) collective-permute-start(bf16[2,7168]{1,0:T(2,128)(2,1)} %gather_fusion.2), channel_id=1, source_target_pairs={{0,32},{32,0},{1,33},{33,1},{2,34},{34,2},{3,35},{35,3},{4,36},{36... | collective-permute-start | bytes 86024 | tf_op jit(solution)/shard_map/ppermute | solution.py:18
  3.5 69.0 %collective-permute-start.4 = (bf16[2,7168]{1,0:T(2,128)(2,1)}, bf16[2,7168]{1,0:T(2,128)(2,1)}, u32[]{:S(2)}, u32[]{:S(2)}) collective-permute-start(bf16[2,7168]{1,0:T(2,128)(2,1)} %gather_fusion.2), channel_id=1, source_target_pairs={{0,64},{64,0},{1,65},{65,1},{2,66},{66,2},{3,67},{67,3},{4,68},{68... | collective-permute-start | bytes 86024 | tf_op jit(solution)/shard_map/ppermute | solution.py:18
  4.2 68.8 %collective-permute-start.5 = (bf16[2,7168]{1,0:T(2,128)(2,1)}, bf16[2,7168]{1,0:T(2,128)(2,1)}, u32[]{:S(2)}, u32[]{:S(2)}) collective-permute-start(bf16[2,7168]{1,0:T(2,128)(2,1)} %gather_fusion.2), channel_id=1, source_target_pairs={{0,96},{32,64},{64,32},{96,0},{1,97},{33,65},{65,33},{97,1},{2,98}... | collective-permute-start | bytes 86024 | tf_op jit(solution)/shard_map/ppermute | solution.py:18
  18.0 14.8 %copy-start.8 = (s32[1,128]{1,0:T(1,128)S(1)}, s32[1,128]{1,0:T(1,128)}, u32[]{:S(2)}) copy-start(s32[1,128]{1,0:T(1,128)} %param.16) | copy-start | bytes 1540
  32.8 4.4 %copy-start.5 = (s32[1,16]{1,0:T(1,128)S(1)}, s32[1,16]{1,0:T(1,128)}, u32[]{:S(2)}) copy-start(s32[1,16]{1,0:T(1,128)} %param.15) | copy-start | bytes 196
  62.5 3.2 copy-start.2
  62.5 3.3 copy-start.3
  62.5 4.2 %copy-start.4 = (s32[1,2]{1,0:T(1,128)S(1)}, s32[1,2]{1,0:T(1,128)}, u32[]{:S(2)}) copy-start(s32[1,2]{1,0:T(1,128)} %param.17) | copy-start | bytes 28
  62.5 4.6 %copy-start.9 = (s32[1,2]{1,0:T(1,128)S(1)}, s32[1,2]{1,0:T(1,128)}, u32[]{:S(2)}) copy-start(s32[1,2]{1,0:T(1,128)} %param.18) | copy-start | bytes 28
  62.5 11.6 %copy-start.1 = (bf16[16,7168]{1,0:T(8,128)(2,1)S(1)}, bf16[16,7168]{1,0:T(8,128)(2,1)}, u32[]{:S(2)}) copy-start(bf16[16,7168]{1,0:T(8,128)(2,1)} %param.14) | copy-start | bytes 688132
  64.6 25.7 %collective-permute-start = (bf16[2,65536]{1,0:T(2,128)(2,1)S(1)}, bf16[2,65536]{1,0:T(2,128)(2,1)S(1)}, u32[]{:S(2)}, u32[]{:S(2)}) collective-permute-start(bf16[2,65536]{1,0:T(2,128)(2,1)S(1)} %gather_fusion.1), channel_id=1, source_target_pairs={{0,32},{32,0},{1,33},{33,1},{2,34},{34,2},{3,35},{35,3},{4,36},{36... | collective-permute-start | bytes 786440 | tf_op jit(solution)/shard_map/ppermute | solution.py:18
  65.0 25.5 %collective-permute-start.1 = (bf16[2,65536]{1,0:T(2,128)(2,1)S(1)}, bf16[2,65536]{1,0:T(2,128)(2,1)S(1)}, u32[]{:S(2)}, u32[]{:S(2)}) collective-permute-start(bf16[2,65536]{1,0:T(2,128)(2,1)S(1)} %gather_fusion.1), channel_id=1, source_target_pairs={{0,64},{64,0},{1,65},{65,1},{2,66},{66,2},{3,67},{67,3},{4,68},{68... | collective-permute-start | bytes 786440 | tf_op jit(solution)/shard_map/ppermute | solution.py:18
  71.5 18.9 %collective-permute-start.2 = (bf16[2,65536]{1,0:T(2,128)(2,1)S(1)}, bf16[2,65536]{1,0:T(2,128)(2,1)S(1)}, u32[]{:S(2)}, u32[]{:S(2)}) collective-permute-start(bf16[2,65536]{1,0:T(2,128)(2,1)S(1)} %gather_fusion.1), channel_id=1, source_target_pairs={{0,96},{32,64},{64,32},{96,0},{1,97},{33,65},{65,33},{97,1},{2,98}... | collective-permute-start | bytes 786440 | tf_op jit(solution)/shard_map/ppermute | solution.py:18
  72.4 134.0 %collective-permute-start.6 = (bf16[7168,256]{1,0:T(8,128)(2,1)}, bf16[7168,256]{1,0:T(8,128)(2,1)}, u32[]{:S(2)}, u32[]{:S(2)}) collective-permute-start(bf16[7168,256]{1,0:T(8,128)(2,1)} %bitcast.82), channel_id=1, source_target_pairs={{0,32},{32,0},{1,33},{33,1},{2,34},{34,2},{3,35},{35,3},{4,36},{36... | collective-permute-start | bytes 11010056 | tf_op jit(solution)/shard_map/ppermute | solution.py:18
  73.0 145.1 %collective-permute-start.7 = (bf16[7168,256]{1,0:T(8,128)(2,1)}, bf16[7168,256]{1,0:T(8,128)(2,1)}, u32[]{:S(2)}, u32[]{:S(2)}) collective-permute-start(bf16[7168,256]{1,0:T(8,128)(2,1)} %bitcast.83), channel_id=1, source_target_pairs={{0,32},{32,0},{1,33},{33,1},{2,34},{34,2},{3,35},{35,3},{4,36},{36... | collective-permute-start | bytes 11010056 | tf_op jit(solution)/shard_map/ppermute | solution.py:18
  79.3 120.9 %all-to-all-start = ((bf16[64,8,7168]{2,1,0:T(8,128)(2,1)}), bf16[64,8,7168]{2,1,0:T(8,128)(2,1)}, u32[]{:S(2)}, u32[]{:S(2)}) async-start(bf16[64,8,7168]{2,1,0:T(8,128)(2,1)} %fusion.1), calls=%async_computation | async-start | bytes 14680064 | tf_op jit(solution)/shard_map/all_to_all | solution.py:98
  90.4 134.2 %collective-permute-start.8 = (bf16[256,7168]{1,0:T(8,128)(2,1)}, bf16[256,7168]{1,0:T(8,128)(2,1)}, u32[]{:S(2)}, u32[]{:S(2)}) collective-permute-start(bf16[256,7168]{1,0:T(8,128)(2,1)} %bitcast.84), channel_id=1, source_target_pairs={{0,32},{32,0},{1,33},{33,1},{2,34},{34,2},{3,35},{35,3},{4,36},{36... | collective-permute-start | bytes 11010056 | tf_op jit(solution)/shard_map/ppermute | solution.py:18
  206.4 6.4 %copy-start.6 = (bf16[1,7168,256]{2,1,0:T(8,128)(2,1)S(1)}, bf16[1,7168,256]{2,1,0:T(8,128)(2,1)}, u32[]{:S(2)}) copy-start(bf16[1,7168,256]{2,1,0:T(8,128)(2,1)} %param.22) | copy-start | bytes 11010052
  218.1 6.4 %copy-start.7 = (bf16[1,256,7168]{2,1,0:T(8,128)(2,1)S(1)}, bf16[1,256,7168]{2,1,0:T(8,128)(2,1)}, u32[]{:S(2)}) copy-start(bf16[1,256,7168]{2,1,0:T(8,128)(2,1)} %param.23) | copy-start | bytes 11010052
  233.8 114.3 %all-to-all-start.1 = ((bf16[64,8,7168]{2,1,0:T(8,128)(2,1)}), bf16[64,8,7168]{2,1,0:T(8,128)(2,1)}, u32[]{:S(2)}, u32[]{:S(2)}) async-start(bf16[64,8,7168]{2,1,0:T(8,128)(2,1)} %fusion.2), calls=%async_computation.1 | async-start | bytes 14680064 | tf_op jit(solution)/shard_map/all_to_all | solution.py:115
  251.3 101.7 %copy-start = (bf16[16,65536]{1,0:T(8,128)(2,1)}, bf16[16,65536]{1,0:T(8,128)(2,1)S(1)}, u32[]{:S(2)}) copy-start(bf16[16,65536]{1,0:T(8,128)(2,1)S(1)} %dynamic_update_slice.7) | copy-start | bytes 6291460
where the time goes:
time: 354 us; the launch traced here: 353 us
  waiting for transfers between devices  206 us (58%)
  local copies, waits for them, and re-layouts  58.4 us (16%)
  matrix products  57.1 us (16%)
  starting transfers between devices  24.1 us (7%)
  between operations  4.8 us (1%)
    all_to_all x1, waiting for transfers between devices, body(): lax.all_to_all(outgoing, PEERS, split_axis=0, concat_axis=0, tiled=True)  109 us
    all_to_all x1, waiting for transfers between devices, body(): lax.all_to_all(partial.reshape(2 * experts, capacity, model_width), PEERS...  96.8 us
    reshape x1, local copies, waits for them, and re-layouts, attend(): pages = latent_pool.reshape(latent_pool.shape[0], -1, kv_width)  14.8 us
    unnamed x24, local copies, waits for them, and re-layouts  14 us
    dot_general x2, matrix products, units(): gate_proj = jnp.dot(arrived, gate, preferred_element_type=jnp.float32)  12.6 us
    gather x1, local copies, waits for them, and re-layouts, attend(): key_cache = pages[page_table.reshape(-1)].reshape(row_count, -1, kv_width)  11.7 us
    dot_general x2, matrix products, units(): up_proj = jnp.dot(arrived, up, preferred_element_type=jnp.float32)  11.6 us
    all_to_all x1, starting transfers between devices, body(): lax.all_to_all(outgoing, PEERS, split_axis=0, concat_axis=0, tiled=True)  11.1 us
  transfers between devices with their start and end apart: 11, of which 2 were waited for; matrix products, arithmetic and copies ran while one was open for 29% of the time, Pallas kernels for 0%

commit v1 on v0

--- a/solution.py
+++ b/solution.py
@@ -95,6 +95,7 @@
         picks, rows, (((0,), (0,)), ((), ())), preferred_element_type=jnp.float32
     )
     outgoing = outgoing.astype(jnp.bfloat16).reshape(2 * experts, capacity, model_width)
+    outgoing, latent_pool, queries = lax.optimization_barrier((outgoing, latent_pool, queries))
     arrived = lax.all_to_all(outgoing, PEERS, split_axis=0, concat_axis=0, tiled=True)
     arrived = arrived.reshape(2 * experts * capacity, model_width)
 
@@ -103,6 +104,7 @@
     down_other = flip(w_down[0], ("core",), 1)
 
     context = attend(latent_pool, queries, lengths, page_table)
+    arrived, context = lax.optimization_barrier((arrived, context))
 
     def units(gate, up):
         gate_proj = jnp.dot(arrived, gate, preferred_element_type=jnp.float32)

time: 354 us -> 302 us (0.85)
  waiting for transfers between devices: 206 us -> 145 us
  matrix products: 57.1 us -> 60.7 us
    all_to_all x1, waiting for transfers between devices: 109 us -> 44.2 us  [body(): lax.all_to_all(outgoing, PEERS, split_axis=0, concat_axis=0, tiled=True)]
    optimization_barrier x0 -> x1, local copies, waits for them, and re-layouts: none -> 12.6 us  [body(): lax.optimization_barrier((outgoing, latent_pool, queries))]
    unnamed x24 -> x15, local copies, waits for them, and re-layouts: 14 us -> 2.71 us
  transfers between devices with their start and end apart: 11 -> 11, of which waited for: 2 -> 2; matrix products, arithmetic and copies ran while one was open for 29% -> 37% of each run, Pallas kernels for 0% -> 0%
where the time goes in v1:
time: 302 us; the launch traced here: 299 us
  waiting for transfers between devices  145 us (48%)
  matrix products  60.7 us (20%)
  local copies, waits for them, and re-layouts  59 us (20%)
  starting transfers between devices  26.4 us (9%)
  between operations  4.86 us (2%)
    all_to_all x1, waiting for transfers between devices, body(): lax.all_to_all(partial.reshape(2 * experts, capacity, model_width), PEERS...  100 us
    all_to_all x1, waiting for transfers between devices, body(): lax.all_to_all(outgoing, PEERS, split_axis=0, concat_axis=0, tiled=True)  44.2 us
    reshape x1, local copies, waits for them, and re-layouts, attend(): pages = latent_pool.reshape(latent_pool.shape[0], -1, kv_width)  14.8 us
    dot_general x2, matrix products, units(): gate_proj = jnp.dot(arrived, gate, preferred_element_type=jnp.float32)  12.8 us
    optimization_barrier x1, local copies, waits for them, and re-layouts, body(): lax.optimization_barrier((outgoing, latent_pool, queries))  12.6 us
    gather x1, local copies, waits for them, and re-layouts, attend(): key_cache = pages[page_table.reshape(-1)].reshape(row_count, -1, kv_width)  11.7 us
    dot_general x2, matrix products, units(): up_proj = jnp.dot(arrived, up, preferred_element_type=jnp.float32)  11.6 us
    all_to_all x1, starting transfers between devices, body(): lax.all_to_all(outgoing, PEERS, split_axis=0, concat_axis=0, tiled=True)  11.2 us
  transfers between devices with their start and end apart: 11, of which 2 were waited for; matrix products, arithmetic and copies ran while one was open for 37% of the time, Pallas kernels for 0%

profile of v1, /device:TPU:58, one launch (start us, length us, event | category | flops | bytes accessed | tf_op | source)
XLA Modules:
  0.0 298.6 jit_solution(6618774087979814443)
XLA Ops:
  0.6 0.7 fusion.31
  1.3 1.6 gather_fusion
  2.9 0.1 collective-permute-start
  3.0 0.8 collective-permute-start.1
  3.8 1.0 collective-permute-start.2
  4.8 0.8 copy.58
  5.6 0.8 copy.67
  6.4 0.1 select_reduce_fusion
  6.5 0.1 copy.59
  6.6 0.1 copy.60
  6.7 0.1 copy.61
  6.8 0.1 copy.62
  6.9 0.1 copy.68
  7.0 0.1 copy.69
  7.1 0.1 eq.80
  7.2 0.7 convert_reduce_fusion.1
  8.0 0.8 fusion.30
  8.8 0.1 broadcast_select_fusion.4
  8.9 0.7 compare_bitcast_fusion
  9.5 0.0 collective-permute-done
  9.6 0.0 collective-permute-done.1
  9.6 0.0 collective-permute-done.2
  9.6 0.1 broadcast_select_fusion.3
  9.7 6.0 %fusion.1 = bf16[64,8,7168]{2,1,0:T(8,128)(2,1)} fusion(bf16[2,7168]{1,0:T(2,128)(2,1)S(1)} %broadcast_select_fusion.3, bf16[16,7168]{1,0:T(8,128)(2,1)} %param.14, bf16[18,256]{1,0:T(8,128)(2,1)S(1)} %maximum_convert_fusion), kind=kOutput, calls=%fused_computation.6 | convolution fusion | flops 136343552 | bytes 7607296 | tf_op jit(solution)/shard_map/dot_general | solution.py:94
  15.7 11.2 %all-to-all-start = ((bf16[64,8,7168]{2,1,0:T(8,128)(2,1)}), bf16[64,8,7168]{2,1,0:T(8,128)(2,1)}, u32[]{:S(2)}, u32[]{:S(2)}) async-start(bf16[64,8,7168]{2,1,0:T(8,128)(2,1)} %fusion.1), calls=%async_computation | async-start | bytes 14680064 | tf_op jit(solution)/shard_map/all_to_all | solution.py:99
  26.9 0.1 collective-permute-start.6
  27.0 0.5 collective-permute-start.7
  27.5 0.1 collective-permute-start.8
  27.6 0.6 fusion.43
  32.1 0.1 iota_compare_fusion.1
  32.2 12.6 %copy.63 = bf16[128,36864]{0,1:T(8,128)(2,1)} copy(bf16[128,36864]{1,0:T(8,128)(2,1)} %param.12) | data formatting | bytes 18874368 | tf_op jit(solution)/shard_map/optimization_barrier | solution.py:98
  44.8 14.8 %copy.64 = bf16[128,64,576]{2,1,0:T(8,128)(2,1)} copy(bf16[128,64,576]{0,2,1:T(8,128)(2,1)} %bitcast.52) | data formatting | bytes 18874368 | tf_op jit(solution)/shard_map/reshape | solution.py:33
  59.5 4.4 %reshape.170 = bf16[16,128,576]{2,1,0:T(8,128)(2,1)S(1)} reshape(bf16[16,73728]{1,0:T(8,128)(2,1)} %param.13) | data formatting | bytes 4718592 | tf_op jit(solution)/shard_map/reshape | solution.py:38
  63.9 11.7 %gather_fusion.1 = bf16[128,64,576]{2,1,0:T(8,128)(2,1)} fusion(bf16[128,64,576]{2,1,0:T(8,128)(2,1)} %copy.64, s32[1024]{0:T(1024)S(1)} %pad_clamp_fusion), kind=kCustom, calls=%fused_computation.1 | custom fusion | bytes 18874880 | tf_op jit(solution)/shard_map/gather | solution.py:34
  75.6 9.6 %fusion.44 = (f32[16,128]{1,0:T(8,128)S(1)}, f32[16,128,512]{2,1,0:T(8,128)}) fusion(pred[16,512]{1,0:T(8,128)(4,1)S(1)} %iota_compare_fusion.1, bf16[16,128,576]{2,1,0:T(8,128)(2,1)S(1)} %reshape.170, bf16[16,512,576]{2,1,0:T(8,128)(2,1)} %bitcast.53), kind=kOutput, calls=%fused_computation.79 | convolution fusion | flops 1212154368 | bytes 16007168 | tf_op jit(solution)/shard_map/sub | solution.py:45
  85.2 6.1 %fusion.14 = bf16[16,128,512]{2,1,0:T(8,128)(2,1)S(1)} fusion(bf16[16,512,576]{2,1,0:T(8,128)(2,1)} %bitcast.54, f32[16,128,512]{2,1,0:T(8,128)} %get-tuple-element.23, f32[16,128]{1,0:T(8,128)S(1)} %get-tuple-element.22), kind=kOutput, calls=%fused_computation.23 | convolution fusion | flops 1076887552 | bytes 14688256 | tf_op jit(solution)/shard_map/rht,rtc->rhc/dot_general | solution.py:47
  91.3 1.2 copy.72
  92.4 44.2 %all-to-all-done = bf16[64,8,7168]{2,1,0:T(8,128)(2,1)} async-done(((bf16[64,8,7168]{2,1,0:T(8,128)(2,1)}), bf16[64,8,7168]{2,1,0:T(8,128)(2,1)}, u32[]{:S(2)}, u32[]{:S(2)}) %all-to-all-start) | async-done | bytes 7340064 | tf_op jit(solution)/shard_map/all_to_all | solution.py:99
  136.7 0.9 gather_fusion.2
  137.6 0.1 collective-permute-start.3
  137.7 2.3 collective-permute-start.4
  139.9 6.4 %fusion.38 = f32[512,256]{0,1:T(8,128)S(1)} fusion(bf16[512,7168]{1,0:T(8,128)(2,1)} %bitcast.8, bf16[1,7168,256]{2,1,0:T(8,128)(2,1)} %param.21), kind=kOutput, calls=%fused_computation.73 | convolution fusion | flops 1879048192 | bytes 11534336 | tf_op jit(solution)/shard_map/dot_general | solution.py:110
  146.3 0.0 copy-start.3
  146.3 0.0 collective-permute-done.6
  146.3 0.4 collective-permute-start.5
  146.7 6.4 %fusion.47 = f32[512,256]{0,1:T(8,128)S(1)} fusion(bf16[512,7168]{1,0:T(8,128)(2,1)} %bitcast.8, bf16[7168,256]{1,0:T(8,128)(2,1)} %collective-permute-done.6), kind=kOutput, calls=%fused_computation.81 | convolution fusion | flops 1879048192 | bytes 11534336 | tf_op jit(solution)/shard_map/dot_general | solution.py:110
  153.1 5.2 %fusion.17 = bf16[512,256]{0,1:T(8,128)(2,1)S(1)} fusion(bf16[512,7168]{1,0:T(8,128)(2,1)} %bitcast.8, f32[512,256]{0,1:T(8,128)S(1)} %fusion.38, bf16[1,7168,256]{2,1,0:T(8,128)(2,1)S(1)} %copy-done.3), kind=kOutput, calls=%fused_computation.25 | convolution fusion | flops 1879834624 | bytes 11796480 | tf_op jit(solution)/shard_map/dot_general | solution.py:111
  158.4 0.0 copy-start.4
  158.4 0.0 collective-permute-done.7
  158.4 6.4 %multiply_convert_fusion = bf16[512,256]{0,1:T(8,128)(2,1)S(1)} fusion(f32[512,256]{0,1:T(8,128)S(1)} %fusion.47, bf16[512,7168]{1,0:T(8,128)(2,1)} %bitcast.8, bf16[7168,256]{1,0:T(8,128)(2,1)} %collective-permute-done.7), kind=kOutput, calls=%fused_computation.29 | convolution fusion | flops 1879834624 | bytes 11796480 | tf_op jit(solution)/shard_map/dot_general | solution.py:111
  164.8 0.0 collective-permute-done.8
  164.8 0.0 copy-done.4
  164.8 9.0 %fusion.2 = bf16[64,8,7168]{2,1,0:T(8,128)(2,1)} fusion(bf16[256,7168]{1,0:T(8,128)(2,1)} %collective-permute-done.8, bf16[256,7168]{1,0:T(8,128)(2,1)S(1)} %bitcast.64, bf16[512,256]{0,1:T(8,128)(2,1)S(1)} %multiply_convert_fusion, bf16[512,256]{0,1:T(8,128)(2,1)S(1)} %fusion.17), kind=kOutput, calls=%fused_computation.7 | convolution fusion | flops 3777495040 | bytes 15204352 | tf_op jit(solution)/shard_map/dot_general | solution.py:116
  173.8 9.9 %all-to-all-start.1 = ((bf16[64,8,7168]{2,1,0:T(8,128)(2,1)}), bf16[64,8,7168]{2,1,0:T(8,128)(2,1)}, u32[]{:S(2)}, u32[]{:S(2)}) async-start(bf16[64,8,7168]{2,1,0:T(8,128)(2,1)} %fusion.2), calls=%async_computation.1 | async-start | bytes 14680064 | tf_op jit(solution)/shard_map/all_to_all | solution.py:117
  183.7 0.0 collective-permute-done.3
  183.7 0.0 collective-permute-done.4
  183.7 0.0 collective-permute-done.5
  183.7 0.5 broadcast_select_fusion.1
  184.2 0.4 fusion.42
  184.6 4.4 %dynamic_update_slice.6 = bf16[16,65536]{1,0:T(8,128)(2,1)S(1)} dynamic-update-slice(bf16[16,65536]{1,0:T(8,128)(2,1)S(1)} %bitcast.56, bf16[1,65536]{1,0:T(2,128)(2,1)S(1)} %get-tuple-element.17, s32[]{:T(128)S(6)} %select_n.57, s32[]{:T(128)} %constant.11.clone.1) | dynamic-update-slice | bytes 262148 | tf_op jit(solution)/shard_map/dynamic_update_slice | solution.py:129
  189.0 4.4 %dynamic_update_slice.7 = bf16[16,65536]{1,0:T(8,128)(2,1)S(1)} dynamic-update-slice(bf16[16,65536]{1,0:T(8,128)(2,1)S(1)} %dynamic_update_slice.6, bf16[1,65536]{1,0:T(2,128)(2,1)S(1)} %get-tuple-element.16, s32[]{:T(128)S(6)} %select_n.58, s32[]{:T(128)} %constant.11.clone.1) | dynamic-update-slice | bytes 262148 | tf_op jit(solution)/shard_map/dynamic_update_slice | solution.py:129
  193.4 0.0 copy-start
  193.4 100.3 %all-to-all-done.1 = bf16[64,8,7168]{2,1,0:T(8,128)(2,1)} async-done(((bf16[64,8,7168]{2,1,0:T(8,128)(2,1)}), bf16[64,8,7168]{2,1,0:T(8,128)(2,1)}, u32[]{:S(2)}, u32[]{:S(2)}) %all-to-all-start.1) | async-done | bytes 7340064 | tf_op jit(solution)/shard_map/all_to_all | solution.py:117
  293.8 4.8 %convolution_convert_fusion.2 = bf16[16,7168]{1,0:T(8,128)(2,1)} fusion(bf16[64,8,7168]{2,1,0:T(8,128)(2,1)} %all-to-all-done.1, bf16[16,256]{1,0:T(8,128)(2,1)S(1)} %get-tuple-element.14), kind=kOutput, calls=%fused_computation.10 | convolution fusion | flops 117587968 | bytes 7577600 | tf_op jit(solution)/shard_map/dot_general | solution.py:125
  (22 shorter events, 0.2 us)
Async XLA Ops:
  2.9 6.7 %collective-permute-start = (bf16[2,7168]{1,0:T(2,128)(2,1)S(1)}, bf16[2,7168]{1,0:T(2,128)(2,1)S(1)}, u32[]{:S(2)}, u32[]{:S(2)}) collective-permute-start(bf16[2,7168]{1,0:T(2,128)(2,1)S(1)} %gather_fusion), channel_id=1, source_target_pairs={{0,32},{32,0},{1,33},{33,1},{2,34},{34,2},{3,35},{35,3},{4,36},{36... | collective-permute-start | bytes 86024 | tf_op jit(solution)/shard_map/ppermute | solution.py:18
  3.0 6.6 %collective-permute-start.1 = (bf16[2,7168]{1,0:T(2,128)(2,1)S(1)}, bf16[2,7168]{1,0:T(2,128)(2,1)S(1)}, u32[]{:S(2)}, u32[]{:S(2)}) collective-permute-start(bf16[2,7168]{1,0:T(2,128)(2,1)S(1)} %gather_fusion), channel_id=1, source_target_pairs={{0,64},{64,0},{1,65},{65,1},{2,66},{66,2},{3,67},{67,3},{4,68},{68... | collective-permute-start | bytes 86024 | tf_op jit(solution)/shard_map/ppermute | solution.py:18
  3.8 5.8 %collective-permute-start.2 = (bf16[2,7168]{1,0:T(2,128)(2,1)S(1)}, bf16[2,7168]{1,0:T(2,128)(2,1)S(1)}, u32[]{:S(2)}, u32[]{:S(2)}) collective-permute-start(bf16[2,7168]{1,0:T(2,128)(2,1)S(1)} %gather_fusion), channel_id=1, source_target_pairs={{0,96},{32,64},{64,32},{96,0},{1,97},{33,65},{65,33},{97,1},{2,98}... | collective-permute-start | bytes 86024 | tf_op jit(solution)/shard_map/ppermute | solution.py:18
  15.7 11.9 %copy-start.1 = (s32[1,2]{1,0:T(1,128)S(1)}, s32[1,2]{1,0:T(1,128)}, u32[]{:S(2)}) copy-start(s32[1,2]{1,0:T(1,128)} %param.17) | copy-start | bytes 28
  15.7 16.4 %copy-start.5 = (s32[1,128]{1,0:T(1,128)S(1)}, s32[1,128]{1,0:T(1,128)}, u32[]{:S(2)}) copy-start(s32[1,128]{1,0:T(1,128)} %param.16) | copy-start | bytes 1540
  15.7 16.4 %copy-start.2 = (s32[1,16]{1,0:T(1,128)S(1)}, s32[1,16]{1,0:T(1,128)}, u32[]{:S(2)}) copy-start(s32[1,16]{1,0:T(1,128)} %param.15) | copy-start | bytes 196
  15.7 121.0 %all-to-all-start = ((bf16[64,8,7168]{2,1,0:T(8,128)(2,1)}), bf16[64,8,7168]{2,1,0:T(8,128)(2,1)}, u32[]{:S(2)}, u32[]{:S(2)}) async-start(bf16[64,8,7168]{2,1,0:T(8,128)(2,1)} %fusion.1), calls=%async_computation | async-start | bytes 14680064 | tf_op jit(solution)/shard_map/all_to_all | solution.py:99
  26.9 119.4 %collective-permute-start.6 = (bf16[7168,256]{1,0:T(8,128)(2,1)}, bf16[7168,256]{1,0:T(8,128)(2,1)}, u32[]{:S(2)}, u32[]{:S(2)}) collective-permute-start(bf16[7168,256]{1,0:T(8,128)(2,1)} %bitcast.61), channel_id=1, source_target_pairs={{0,32},{32,0},{1,33},{33,1},{2,34},{34,2},{3,35},{35,3},{4,36},{36... | collective-permute-start | bytes 11010056 | tf_op jit(solution)/shard_map/ppermute | solution.py:18
  27.0 131.4 %collective-permute-start.7 = (bf16[7168,256]{1,0:T(8,128)(2,1)}, bf16[7168,256]{1,0:T(8,128)(2,1)}, u32[]{:S(2)}, u32[]{:S(2)}) collective-permute-start(bf16[7168,256]{1,0:T(8,128)(2,1)} %bitcast.62), channel_id=1, source_target_pairs={{0,32},{32,0},{1,33},{33,1},{2,34},{34,2},{3,35},{35,3},{4,36},{36... | collective-permute-start | bytes 11010056 | tf_op jit(solution)/shard_map/ppermute | solution.py:18
  27.5 137.3 %collective-permute-start.8 = (bf16[256,7168]{1,0:T(8,128)(2,1)}, bf16[256,7168]{1,0:T(8,128)(2,1)}, u32[]{:S(2)}, u32[]{:S(2)}) collective-permute-start(bf16[256,7168]{1,0:T(8,128)(2,1)} %bitcast.63), channel_id=1, source_target_pairs={{0,32},{32,0},{1,33},{33,1},{2,34},{34,2},{3,35},{35,3},{4,36},{36... | collective-permute-start | bytes 11010056 | tf_op jit(solution)/shard_map/ppermute | solution.py:18
  137.6 46.1 %collective-permute-start.3 = (bf16[2,65536]{1,0:T(2,128)(2,1)S(1)}, bf16[2,65536]{1,0:T(2,128)(2,1)S(1)}, u32[]{:S(2)}, u32[]{:S(2)}) collective-permute-start(bf16[2,65536]{1,0:T(2,128)(2,1)S(1)} %gather_fusion.2), channel_id=1, source_target_pairs={{0,32},{32,0},{1,33},{33,1},{2,34},{34,2},{3,35},{35,3},{4,36},{36... | collective-permute-start | bytes 786440 | tf_op jit(solution)/shard_map/ppermute | solution.py:18
  137.7 46.0 %collective-permute-start.4 = (bf16[2,65536]{1,0:T(2,128)(2,1)S(1)}, bf16[2,65536]{1,0:T(2,128)(2,1)S(1)}, u32[]{:S(2)}, u32[]{:S(2)}) collective-permute-start(bf16[2,65536]{1,0:T(2,128)(2,1)S(1)} %gather_fusion.2), channel_id=1, source_target_pairs={{0,64},{64,0},{1,65},{65,1},{2,66},{66,2},{3,67},{67,3},{4,68},{68... | collective-permute-start | bytes 786440 | tf_op jit(solution)/shard_map/ppermute | solution.py:18
  146.3 6.8 %copy-start.3 = (bf16[1,7168,256]{2,1,0:T(8,128)(2,1)S(1)}, bf16[1,7168,256]{2,1,0:T(8,128)(2,1)}, u32[]{:S(2)}) copy-start(bf16[1,7168,256]{2,1,0:T(8,128)(2,1)} %param.22) | copy-start | bytes 11010052
  146.3 37.4 %collective-permute-start.5 = (bf16[2,65536]{1,0:T(2,128)(2,1)S(1)}, bf16[2,65536]{1,0:T(2,128)(2,1)S(1)}, u32[]{:S(2)}, u32[]{:S(2)}) collective-permute-start(bf16[2,65536]{1,0:T(2,128)(2,1)S(1)} %gather_fusion.2), channel_id=1, source_target_pairs={{0,96},{32,64},{64,32},{96,0},{1,97},{33,65},{65,33},{97,1},{2,98}... | collective-permute-start | bytes 786440 | tf_op jit(solution)/shard_map/ppermute | solution.py:18
  158.4 6.4 %copy-start.4 = (bf16[1,256,7168]{2,1,0:T(8,128)(2,1)S(1)}, bf16[1,256,7168]{2,1,0:T(8,128)(2,1)}, u32[]{:S(2)}) copy-start(bf16[1,256,7168]{2,1,0:T(8,128)(2,1)} %param.23) | copy-start | bytes 11010052
  173.8 120.0 %all-to-all-start.1 = ((bf16[64,8,7168]{2,1,0:T(8,128)(2,1)}), bf16[64,8,7168]{2,1,0:T(8,128)(2,1)}, u32[]{:S(2)}, u32[]{:S(2)}) async-start(bf16[64,8,7168]{2,1,0:T(8,128)(2,1)} %fusion.2), calls=%async_computation.1 | async-start | bytes 14680064 | tf_op jit(solution)/shard_map/all_to_all | solution.py:117
  193.4 105.2 %copy-start = (bf16[16,65536]{1,0:T(8,128)(2,1)}, bf16[16,65536]{1,0:T(8,128)(2,1)S(1)}, u32[]{:S(2)}) copy-start(bf16[16,65536]{1,0:T(8,128)(2,1)S(1)} %dynamic_update_slice.7) | copy-start | bytes 6291460

commit v2 on v0

v2 whole, which is shorter than its diff:
```python
import jax
import jax.numpy as jnp
from jax import lax
from jax.experimental import pallas as pl
from jax.experimental.pallas import tpu as pltpu
from jax.sharding import Mesh, PartitionSpec as P

HEADS = 128
ROPE = 64
TOP = 8
OUT_A = 3584
BACK_A = 3584
STEP = 896

score_scale = 192.0 ** (-0.5)
gain_step = 0.0625

ALL = ("yl", "core", "x", "yh", "z")
PEERS = ("yl", "x", "yh", "z")


def flip(value, axes, mask):
    return lax.ppermute(value, axes, [(i, i ^ mask) for i in range(4 if len(axes) == 2 else 2)])


def swapped(rows, flips):
    by_one = flip(rows, ("core",), 1)
    by_two = flip(rows, ("yl",), 1)
    by_three = flip(rows, ("yl", "core"), 3)
    which = flips.reshape((-1,) + (1,) * (rows.ndim - 1))
    return jnp.where(which == 1, by_one, jnp.where(which == 2, by_two, by_three))


def pairs_of(latent_pool, page_table, row_count, kv_width):
    pages = latent_pool.reshape(latent_pool.shape[0], -1, 2 * kv_width)
    return pages[page_table.reshape(-1)].reshape(row_count, -1, 2 * kv_width)


def halves(pairs, kv_width):
    wide = -(-kv_width // 128) * 128
    return pairs[:, :, :wide], pairs[:, :, 2 * kv_width - wide :]


def probabilities(pairs, query_heads, lengths):
    row_count, _, kv_width = query_heads.shape
    even, odd = halves(pairs, kv_width)
    extra = ((0, 0), (0, 0), (0, even.shape[2] - kv_width))
    at = 2 * lax.broadcasted_iota(jnp.int32, (1, 1, pairs.shape[1]), 2)
    length = lengths.reshape(row_count, 1, 1)

    def scores_of(keys, padded, at):
        scores = jnp.einsum("rhc,rtc->rht", padded, keys, preferred_element_type=jnp.float32)
        return jnp.where(at < length, scores * score_scale, -1e30)

    scores_even = scores_of(even, jnp.pad(query_heads, extra), at)
    scores_odd = scores_of(odd, jnp.pad(query_heads, [pad[::-1] for pad in extra]), at + 1)
    row_max = jnp.maximum(
        jnp.max(scores_even, axis=2, keepdims=True), jnp.max(scores_odd, axis=2, keepdims=True)
    )
    weights_even, weights_odd = jnp.exp(scores_even - row_max), jnp.exp(scores_odd - row_max)
    total = jnp.sum(weights_even, axis=2, keepdims=True)
    total = total + jnp.sum(weights_odd, axis=2, keepdims=True)
    return (weights_even / total).astype(jnp.bfloat16), (weights_odd / total).astype(jnp.bfloat16)


def contexts(probs, pairs, kv_width):
    row_count = pairs.shape[0]
    latent_width = kv_width - ROPE
    even, odd = halves(pairs, kv_width)
    first = even.shape[2] - kv_width

    def mean(probs, keys):
        return jnp.einsum("rht,rtc->rhc", probs, keys, preferred_element_type=jnp.float32)

    context = mean(probs[0], even[:, :, :latent_width])
    context = context + mean(probs[1], odd)[:, :, first : first + latent_width]
    return context.astype(jnp.bfloat16).reshape(row_count, HEADS * latent_width)


def finish_kernel(steps, x, gates, ups, shares, downs, back, activated, sums):
    at = pl.program_id(0)

    @pl.when(at == 0)
    def _():
        for total, share in zip(sums, shares):
            total[...] = share[...]

    @pl.when(at < steps)
    def _():
        for total, w in zip(sums, gates + ups):
            total[...] += jnp.dot(x[...], w[...], preferred_element_type=jnp.float32)

    @pl.when(at == steps - 1)
    def _():
        width = sums[0].shape[1]
        for core in range(2):
            unit = jax.nn.silu(sums[core][...]) * sums[2 + core][...]
            activated[:, core * width : (core + 1) * width] = unit.astype(jnp.bfloat16)

    @pl.when(at >= steps)
    def _():
        width = sums[0].shape[1]
        back[...] = (
            jnp.dot(activated[:, :width], downs[0][...], preferred_element_type=jnp.float32)
            + jnp.dot(activated[:, width:], downs[1][...], preferred_element_type=jnp.float32)
        ).astype(jnp.bfloat16)


def finish(come, gates, ups, shares, downs, first, columns):
    places, rest = come.shape
    units = gates[0].shape[1]
    steps, tail = rest // STEP, columns // STEP

    def kernel(*refs):
        x, *refs = refs
        finish_kernel(
            steps, x, refs[0:2], refs[2:4], refs[4:8], refs[8:10], refs[10], refs[11], refs[12:]
        )

    weight = pl.BlockSpec(
        (STEP, units), lambda i: (first // STEP + jnp.minimum(i, steps - 1), 0)
    )
    share = pl.BlockSpec((places, units), lambda i: (0, 0))
    down = pl.BlockSpec((units, STEP), lambda i: (0, jnp.maximum(i - steps, 0)))
    work = 2 * places * 2 * units
    return pl.pallas_call(
        kernel,
        grid=(steps + tail,),
        in_specs=[pl.BlockSpec((places, STEP), lambda i: (0, jnp.minimum(i, steps - 1)))]
        + [weight] * 4
        + [share] * 4
        + [down] * 2,
        out_specs=[
            pl.BlockSpec((places, STEP), lambda i: (0, jnp.maximum(i - steps, 0))),
            pl.BlockSpec((places, 2 * units), lambda i: (0, 0)),
        ],
        out_shape=[
            jax.ShapeDtypeStruct((places, columns), jnp.bfloat16),
            jax.ShapeDtypeStruct((places, 2 * units), jnp.bfloat16),
        ],
        scratch_shapes=[pltpu.VMEM((places, units), jnp.float32)] * 4,
        compiler_params=pltpu.CompilerParams(vmem_limit_bytes=58 * 1024 * 1024),
        cost_estimate=pl.CostEstimate(
            flops=work * (2 * rest + columns),
            bytes_accessed=2 * (rest * (places + 4 * units) + columns * (places + 2 * units)),
            transcendentals=2 * places * units,
        ),
    )(come, *gates, *ups, *shares, *downs)


def body(
    latent_pool,
    queries,
    hidden,
    lengths,
    page_table,
    send_slot,
    match,
    routes,
    route_gain,
    w_gate,
    w_up,
    w_down,
):
    experts = 32
    row_count = queries.shape[0]
    model_width = hidden.shape[1]
    out_slots = send_slot.reshape(-1)
    flips = match.reshape(-1)

    arriving = swapped(hidden[out_slots], flips)
    slots = jnp.arange(row_count, dtype=jnp.int32)
    leaving = (slots[:, None] == out_slots[None, :]).astype(jnp.float32)
    staying = 1.0 - jnp.sum(leaving, axis=1)

    capacity = min(row_count, max(2, 2 * row_count * TOP // experts))
    expert_ids = jnp.arange(experts, dtype=jnp.int32)
    named = (routes[:, :, None] == expert_ids).astype(jnp.int32)
    chosen = jnp.sum(named, axis=1)
    rank = jnp.cumsum(chosen, axis=0) - chosen
    gain_of = jnp.sum(named * route_gain[:, :, None], axis=1).astype(jnp.float32) * gain_step
    at_slot = (rank[:, :, None] == jnp.arange(capacity, dtype=jnp.int32)) & (chosen[:, :, None] > 0)
    table = at_slot.astype(jnp.float32).reshape(row_count, experts * capacity)
    gain_table = jnp.where(at_slot, gain_of[:, :, None], 0.0).reshape(row_count, experts * capacity)

    places = 2 * experts * capacity
    picks = jnp.concatenate([table * staying[:, None], jnp.dot(leaving.T, table)], axis=0)
    picks = jnp.concatenate([picks, picks], axis=1).astype(jnp.bfloat16)
    rows = jnp.concatenate([hidden, arriving], axis=0)

    def leave(cut):
        out = lax.dot_general(
            picks, cut, (((0,), (0,)), ((), ())), preferred_element_type=jnp.float32
        )
        return out.astype(jnp.bfloat16)

    def exchange(blocks):
        blocks = blocks.reshape(2 * experts, capacity, -1)
        out = lax.all_to_all(blocks, PEERS, split_axis=0, concat_axis=0, tiled=True)
        return out.reshape(places, -1)

    def product(a, b):
        return jnp.dot(a, b, preferred_element_type=jnp.float32)

    gates = (w_gate[0], flip(w_gate[0], ("core",), 1))
    ups = (w_up[0], flip(w_up[0], ("core",), 1))
    downs = (w_down[0], flip(w_down[0], ("core",), 1))
    mix = jnp.concatenate([gain_table, gain_table], axis=1).astype(jnp.bfloat16)

    kv_width = queries.shape[1] // HEADS
    leave_a = leave(rows[:, :OUT_A])
    leave_a, latent_pool, queries = lax.optimization_barrier((leave_a, latent_pool, queries))
    come_a = exchange(leave_a)
    leave_b = leave(rows[:, OUT_A:])
    pairs = pairs_of(latent_pool, page_table, row_count, kv_width)
    query_heads = queries.reshape(row_count, HEADS, kv_width)
    come_a, leave_b = lax.optimization_barrier((come_a, leave_b))
    come_b = exchange(leave_b)
    shares = [product(come_a, w[:OUT_A]) for w in gates + ups]
    probs = probabilities(pairs, query_heads, lengths)
    context = contexts(probs, pairs, kv_width)
    moving = context[out_slots]
    come_b, shares, context, moving = lax.optimization_barrier((come_b, shares, context, moving))
    back_a, activated = finish(come_b, gates, ups, shares, downs, OUT_A, BACK_A)
    back_a, activated = lax.optimization_barrier((back_a, activated))
    final_a = exchange(back_a)
    joined = jnp.concatenate([w[:, BACK_A:] for w in downs], axis=0)
    back_b = product(activated, joined).astype(jnp.bfloat16)
    back = swapped(moving, flips)
    final_a, back_b, context, back = lax.optimization_barrier((final_a, back_b, context, back))
    final_b = exchange(back_b)
    for k in range(out_slots.shape[0]):
        context = lax.dynamic_update_slice_in_dim(context, back[k : k + 1], out_slots[k], 0)
    moe_a = product(mix, final_a).astype(jnp.bfloat16)
    moe_b = product(mix, final_b).astype(jnp.bfloat16)
    return (context, jnp.concatenate([moe_a, moe_b], axis=1))


def solution(mesh):
    fine = Mesh(mesh.devices.reshape(2, 2, 4, 2, 4), ALL)
    rows = P(ALL, None)
    column = ("x", "yh", "z")
    replica = ("yl", "core")
    placed = (
        rows,
        rows,
        rows,
        rows,
        rows,
        rows,
        P(column, None),
        rows,
        rows,
        P(column, None, replica),
        P(column, None, replica),
        P(column, replica, None),
    )
    return jax.shard_map(body, mesh=fine, in_specs=placed, out_specs=(rows, rows), check_vma=False)
```

time: 354 us -> 266 us (0.75)
  waiting for transfers between devices: 206 us -> 90.8 us
  starting transfers between devices: 24.1 us -> 46.9 us
  Pallas kernels: 0 us -> 14.3 us
  local copies, waits for them, and re-layouts: 58.4 us -> 45.8 us
  other arithmetic: 2.43 us -> 6.83 us
    all_to_all x2 -> x4, waiting for transfers between devices: 206 us -> 90.8 us  [exchange(): out = lax.all_to_all(blocks, PEERS, split_axis=0, concat_axis=0, tiled=True)]
    all_to_all x2 -> x4, starting transfers between devices: 19.3 us -> 42.4 us  [exchange(): out = lax.all_to_all(blocks, PEERS, split_axis=0, concat_axis=0, tiled=True)]
    reshape x2 -> x1, local copies, waits for them, and re-layouts: 19.2 us -> 4.38 us  [body(): query_heads = queries.reshape(row_count, HEADS, kv_width)]
    pallas_call x0 -> x1, Pallas kernels: none -> 14.3 us  [finish(): pl.pallas_call(kernel, grid=(steps + tail,), in_specs=[pl.BlockSpec((plac...]
    sub x1 -> x0, matrix products: 7.43 us -> none  [attend(): weights = jnp.exp(scores - row_max)]
    slice x0 -> x2, local copies, waits for them, and re-layouts: none -> 5.69 us  [body(): joined = jnp.concatenate([w[:, BACK_A:] for w in downs], axis=0)]
    dot_general x8 -> x13, matrix products: 49.5 us -> 53 us  [the longest x7 29.9 us: product(): return jnp.dot(a, b, preferred_element_type=jnp.float32)]
    unnamed x24 -> x22, local copies, waits for them, and re-layouts: 14 us -> 11.9 us
  transfers between devices with their start and end apart: 11 -> 13, of which waited for: 2 -> 4; matrix products, arithmetic and copies ran while one was open for 29% -> 37% of each run, Pallas kernels for 0% -> 5%
where the time goes in v2:
time: 266 us; the launch traced here: 263 us
  waiting for transfers between devices  90.8 us (34%)
  matrix products  53.8 us (20%)
  starting transfers between devices  46.9 us (18%)
  local copies, waits for them, and re-layouts  45.8 us (17%)
  Pallas kernels  14.3 us (5%)
  other arithmetic  6.83 us (3%)
  between operations  4.86 us (2%)
    all_to_all x4, waiting for transfers between devices, exchange(): out = lax.all_to_all(blocks, PEERS, split_axis=0, concat_axis=0, tiled=True)  90.8 us
    all_to_all x4, starting transfers between devices, exchange(): out = lax.all_to_all(blocks, PEERS, split_axis=0, concat_axis=0, tiled=True)  42.4 us
    dot_general x7, matrix products, product(): return jnp.dot(a, b, preferred_element_type=jnp.float32)  29.9 us
    pallas_call x1, Pallas kernels, finish(): pl.pallas_call(kernel, grid=(steps + tail,), in_specs=[pl.BlockSpec((plac...  14.3 us
    unnamed x22, local copies, waits for them, and re-layouts  11.9 us
    gather x1, local copies, waits for them, and re-layouts, pairs_of(): return pages[page_table.reshape(-1)].reshape(row_count, -1, 2 * kv_width)  11 us
    dynamic_update_slice x2, local copies, waits for them, and re-layouts, body(): lax.dynamic_update_slice_in_dim(context, back[k:k + 1], out_slots[k], 0)  8.86 us
    dot_general x2, matrix products, scores_of(): jnp.einsum('rhc,rtc->rht', padded, keys, preferred_element_type=jnp.float32)  8.78 us
  transfers between devices with their start and end apart: 13, of which 4 were waited for; matrix products, arithmetic and copies ran while one was open for 37% of the time, Pallas kernels for 5%

profile of v2, /device:TPU:58, one launch (start us, length us, event | category | flops | bytes accessed | tf_op | source)
XLA Modules:
  0.0 263.3 jit_solution(11702845307393245043)
XLA Ops:
  0.6 0.7 fusion.44
  1.3 1.6 gather_fusion
  2.9 0.1 collective-permute-start
  3.0 0.8 collective-permute-start.1
  3.8 1.0 collective-permute-start.2
  4.8 0.8 copy.36
  5.6 0.8 copy.41
  6.4 0.1 select_reduce_fusion
  6.5 0.1 copy.37
  6.6 0.1 copy.38
  6.7 0.1 copy.39
  6.8 0.1 copy.40
  6.9 0.1 copy.42
  7.0 0.1 copy.43
  7.1 0.1 eq.80
  7.2 0.7 convert_reduce_fusion.1
  8.0 0.8 fusion.43
  8.8 0.1 broadcast_select_fusion.4
  8.9 0.7 compare_bitcast_fusion
  9.6 0.1 broadcast_select_fusion.3
  9.7 3.9 %convolution_convert_fusion.2 = bf16[512,3584]{1,0:T(8,128)(2,1)} fusion(bf16[16,7168]{1,0:T(8,128)(2,1)} %param.14, bf16[2,7168]{1,0:T(2,128)(2,1)S(1)} %broadcast_select_fusion.3, bf16[18,256]{1,0:T(8,128)(2,1)S(1)} %maximum_convert_fusion), kind=kOutput, calls=%fused_computation.5 | convolution fusion | flops 68190208 | bytes 3937280 | tf_op jit(solution)/shard_map/dot_general | solution.py:192
  13.6 11.1 %all-to-all-start = ((bf16[64,8,3584]{2,1,0:T(8,128)(2,1)}), bf16[64,8,3584]{2,1,0:T(8,128)(2,1)}, u32[]{:S(2)}, u32[]{:S(2)}) async-start(bf16[64,8,3584]{2,1,0:T(8,128)(2,1)} %bitcast.54), calls=%async_computation | async-start | bytes 7340032 | tf_op jit(solution)/shard_map/all_to_all | solution.py:199
  24.7 0.0 copy-start.8
  24.7 0.0 copy-start.7
  24.7 0.1 collective-permute-start.4
  24.8 0.5 collective-permute-start.3
  25.3 0.1 collective-permute-start.5
  25.4 2.8 %slice.93 = bf16[256,3584]{1,0:T(8,128)(2,1)} slice(bf16[256,7168]{1,0:T(8,128)(2,1)} %bitcast.64), slice={[0:256], [3584:7168]} | slice | bytes 3670016 | tf_op jit(solution)/shard_map/slice | solution.py:227
  28.2 0.6 fusion.59
  32.8 0.1 broadcast_compare_fusion
  32.8 9.2 %copy.44 = bf16[16,8,32,1152]{3,2,1,0:T(8,128)(2,1)} copy(bf16[16,8,32,1152]{3,1,2,0:T(8,128)(2,1)} %bitcast.56) | data formatting | bytes 18874368
  42.0 4.4 %reshape.247 = bf16[16,128,576]{2,1,0:T(8,128)(2,1)S(1)} reshape(bf16[16,73728]{1,0:T(8,128)(2,1)} %param.13) | data formatting | bytes 4718592 | tf_op jit(solution)/shard_map/reshape | solution.py:216
  46.4 11.0 %gather_fusion.1 = bf16[128,32,1152]{2,1,0:T(8,128)(2,1)} fusion(bf16[128,32,1152]{2,1,0:T(8,128)(2,1)} %bitcast.53, s32[1024]{0:T(1024)S(1)} %pad_clamp_fusion), kind=kCustom, calls=%fused_computation.1 | custom fusion | bytes 18874880 | tf_op jit(solution)/shard_map/gather | solution.py:36
  57.4 5.8 %fusion.16 = (f32[16,128]{1,0:T(8,128)S(1)}, f32[16,128,256]{2,1,0:T(8,128)}) fusion(pred[16,256]{1,0:T(8,128)(4,1)S(1)} %get-tuple-element.49, bf16[16,256,1152]{2,1,0:T(8,128)(2,1)} %bitcast.57, bf16[16,128,576]{2,1,0:T(8,128)(2,1)S(1)} %reshape.247), kind=kOutput, calls=%fused_computation.29 | convolution fusion | flops 672659456 | bytes 9711616 | tf_op jit(solution)/shard_map/rhc,rtc->rht/dot_general | solution.py:52
  63.1 3.0 %fusion.17 = (f32[16,128]{1,0:T(8,128)S(1)}, f32[16,128,256]{2,1,0:T(8,128)}) fusion(pred[16,256]{1,0:T(8,128)(4,1)S(1)} %get-tuple-element.48, bf16[16,256,1152]{2,1,0:T(8,128)(2,1)S(1)} %bitcast.60, bf16[16,128,576]{2,1,0:T(8,128)(2,1)S(1)} %reshape.247), kind=kOutput, calls=%fused_computation.30 | convolution fusion | flops 672659456 | bytes 9973760 | tf_op jit(solution)/shard_map/rhc,rtc->rht/dot_general | solution.py:52
  66.2 2.9 %convolution_convert_fusion.1 = bf16[512,3584]{1,0:T(8,128)(2,1)} fusion(bf16[2,7168]{1,0:T(2,128)(2,1)S(1)} %broadcast_select_fusion.3, bf16[16,7168]{1,0:T(8,128)(2,1)S(1)} %copy-done.5, bf16[18,256]{1,0:T(8,128)(2,1)S(1)} %maximum_convert_fusion), kind=kOutput, calls=%fused_computation.4 | convolution fusion | flops 68190208 | bytes 3937280 | tf_op jit(solution)/shard_map/dot_general | solution.py:192
  69.1 2.9 %all-to-all-done = bf16[64,8,3584]{2,1,0:T(8,128)(2,1)} async-done(((bf16[64,8,3584]{2,1,0:T(8,128)(2,1)}), bf16[64,8,3584]{2,1,0:T(8,128)(2,1)}, u32[]{:S(2)}, u32[]{:S(2)}) %all-to-all-start) | async-done | bytes 3670048 | tf_op jit(solution)/shard_map/all_to_all | solution.py:199
  72.0 10.4 %all-to-all-start.1 = ((bf16[64,8,3584]{2,1,0:T(8,128)(2,1)}), bf16[64,8,3584]{2,1,0:T(8,128)(2,1)}, u32[]{:S(2)}, u32[]{:S(2)}) async-start(bf16[64,8,3584]{2,1,0:T(8,128)(2,1)} %bitcast.55), calls=%async_computation.1 | async-start | bytes 7340032 | tf_op jit(solution)/shard_map/all_to_all | solution.py:199
  82.4 3.1 %fusion.29 = (f32[16,128]{1,0:T(8,128)S(1)}, f32[16,128]{1,0:T(8,128)S(1)}) fusion(f32[16,128,256]{2,1,0:T(8,128)} %get-tuple-element.55, f32[16,128]{1,0:T(8,128)S(1)} %max.8, pred[16,256]{1,0:T(8,128)(4,1)S(1)} %get-tuple-element.48, f32[16,128,256]{2,1,0:T(8,128)S(1)} %copy-done.3, pred[16,256]{1,0:T(8,128)(4,1)S(1)} %get-tuple-element.49), kind=kLoop, calls=%fused_computation.42 | loop fusion | flops 4190208 | bytes 4227072 | tf_op jit(solution)/shard_map/reduce_sum | solution.py:62
  85.5 4.1 %fusion.4 = f32[16,128,512]{2,1,0:T(8,128)S(1)} fusion(bf16[16,256,1152]{2,1,0:T(8,128)(2,1)} %bitcast.58, f32[16,128,256]{2,1,0:T(8,128)S(1)} %copy-done.4, f32[16,128]{1,0:T(8,128)S(1)} %add.61, f32[16,128]{1,0:T(8,128)S(1)} %max.8, pred[16,256]{1,0:T(8,128)(4,1)S(1)} %get-tuple-element.48), kind=kOutput, calls=%fused_computation.12 | convolution fusion | flops 539492352 | bytes 10506240 | tf_op jit(solution)/shard_map/rht,rtc->rhc/dot_general | solution.py:73
  89.7 3.3 %add_convert_fusion = bf16[16,128,512]{2,1,0:T(8,128)(2,1)S(1)} fusion(f32[16,128,512]{2,1,0:T(8,128)S(1)} %fusion.4, bf16[16,256,1152]{2,1,0:T(8,128)(2,1)} %bitcast.59, f32[16,128,256]{2,1,0:T(8,128)S(1)} %copy-done.3, f32[16,128]{1,0:T(8,128)S(1)} %add.61, f32[16,128]{1,0:T(8,128)S(1)} %max.8, pred[16,256]{1,0:T(8,128)(4,1)S(1)} %get-tuple-element.49), kind=kOutput, calls=%fused_computation.16 | convolution fusion | flops 541589504 | bytes 12603392 | tf_op jit(solution)/shard_map/rht,rtc->rhc/dot_general | solution.py:73
  93.0 1.2 copy.45
  94.2 0.9 gather_fusion.2
  95.1 4.7 %fusion.22.refs_7_ = f32[512,256]{1,0:T(8,128)} fusion(bf16[512,3584]{1,0:T(8,128)(2,1)} %bitcast.8, bf16[1,7168,256]{2,1,0:T(8,128)(2,1)} %param.22), kind=kOutput, calls=%fused_computation.35 | convolution fusion | flops 939524096 | bytes 6029312 | tf_op jit(solution)/shard_map/dot_general | solution.py:203
  99.8 4.0 %fusion.24.refs_5_ = f32[512,256]{1,0:T(8,128)} fusion(bf16[512,3584]{1,0:T(8,128)(2,1)} %bitcast.8, bf16[1,7168,256]{2,1,0:T(8,128)(2,1)S(1)} %copy-done.2), kind=kOutput, calls=%fused_computation.37 | convolution fusion | flops 939524096 | bytes 6029312 | tf_op jit(solution)/shard_map/dot_general | solution.py:203
  103.8 2.8 %slice.94 = bf16[256,3584]{1,0:T(8,128)(2,1)} slice(bf16[256,7168]{1,0:T(8,128)(2,1)} %collective-permute-done.5.refs_10_), slice={[0:256], [3584:7168]} | slice | bytes 3670016 | tf_op jit(solution)/shard_map/slice | solution.py:227
  106.6 4.5 %fusion.18.refs_8_ = f32[512,256]{1,0:T(8,128)} fusion(bf16[512,3584]{1,0:T(8,128)(2,1)} %bitcast.8, bf16[7168,256]{1,0:T(8,128)(2,1)} %collective-permute-done.4.refs_4_), kind=kOutput, calls=%fused_computation.31 | convolution fusion | flops 939524096 | bytes 6029312 | tf_op jit(solution)/shard_map/dot_general | solution.py:203
  111.1 4.6 %fusion.20.refs_6_ = f32[512,256]{1,0:T(8,128)} fusion(bf16[512,3584]{1,0:T(8,128)(2,1)} %bitcast.8, bf16[7168,256]{1,0:T(8,128)(2,1)} %collective-permute-done.3.refs_2_), kind=kOutput, calls=%fused_computation.33 | convolution fusion | flops 939524096 | bytes 6029312 | tf_op jit(solution)/shard_map/dot_general | solution.py:203
  115.7 13.5 %all-to-all-done.1 = bf16[64,8,3584]{2,1,0:T(8,128)(2,1)} async-done(((bf16[64,8,3584]{2,1,0:T(8,128)(2,1)}), bf16[64,8,3584]{2,1,0:T(8,128)(2,1)}, u32[]{:S(2)}, u32[]{:S(2)}) %all-to-all-start.1) | async-done | bytes 3670048 | tf_op jit(solution)/shard_map/all_to_all | solution.py:199
  129.2 0.8 collective-permute-start.7
  129.9 1.1 collective-permute-start.8
  131.0 14.3 %shard_map.131 = (bf16[512,3584]{1,0:T(8,128)(2,1)}, bf16[512,512]{1,0:T(8,128)(2,1)}) custom-call(bf16[512,3584]{1,0:T(8,128)(2,1)} %bitcast.10.refs_0_, bf16[7168,256]{1,0:T(8,128)(2,1)} %bitcast.69, bf16[7168,256]{1,0:T(8,128)(2,1)} %collective-permute-done.3.refs_2_, bf16[7168,256]{1,0:T(8,128)(2,1)} %bitcast.71, ...), custom_call_target="tpu_custom_call" | custom-call | flops 5637144576 | bytes 18350080 | tf_op jit(solution)/shard_map/pallas_call | solution.py:126
  145.3 11.1 %all-to-all-start.2 = ((bf16[64,8,3584]{2,1,0:T(8,128)(2,1)}), bf16[64,8,3584]{2,1,0:T(8,128)(2,1)}, u32[]{:S(2)}, u32[]{:S(2)}) async-start(bf16[64,8,3584]{2,1,0:T(8,128)(2,1)} %bitcast.67), calls=%async_computation.2 | async-start | bytes 7340032 | tf_op jit(solution)/shard_map/all_to_all | solution.py:199
  156.5 6.1 %convolution_convert_fusion = bf16[512,3584]{1,0:T(8,128)(2,1)} fusion(bf16[512,512]{1,0:T(8,128)(2,1)} %get-tuple-element.31, bf16[256,3584]{1,0:T(8,128)(2,1)} %slice.94, bf16[256,3584]{1,0:T(8,128)(2,1)} %slice.93), kind=kOutput, calls=%fused_computation.3 | convolution fusion | flops 1888223232 | bytes 7864320 | tf_op jit(solution)/shard_map/dot_general | solution.py:203
  162.6 0.5 broadcast_select_fusion.1
  163.1 41.0 %all-to-all-done.2 = bf16[64,8,3584]{2,1,0:T(8,128)(2,1)} async-done(((bf16[64,8,3584]{2,1,0:T(8,128)(2,1)}), bf16[64,8,3584]{2,1,0:T(8,128)(2,1)}, u32[]{:S(2)}, u32[]{:S(2)}) %all-to-all-start.2) | async-done | bytes 3670048 | tf_op jit(solution)/shard_map/all_to_all | solution.py:199
  204.1 9.9 %all-to-all-start.3 = ((bf16[64,8,3584]{2,1,0:T(8,128)(2,1)}), bf16[64,8,3584]{2,1,0:T(8,128)(2,1)}, u32[]{:S(2)}, u32[]{:S(2)}) async-start(bf16[64,8,3584]{2,1,0:T(8,128)(2,1)} %bitcast.66), calls=%async_computation.3 | async-start | bytes 7340032 | tf_op jit(solution)/shard_map/all_to_all | solution.py:199
  214.0 0.4 fusion.58
  214.3 4.4 %dynamic_update_slice.6 = bf16[16,65536]{1,0:T(8,128)(2,1)S(1)} dynamic-update-slice(bf16[16,65536]{1,0:T(8,128)(2,1)S(1)} %bitcast.62, bf16[1,65536]{1,0:T(2,128)(2,1)S(1)} %get-tuple-element.45, s32[]{:T(128)S(6)} %select_n.61, s32[]{:T(128)} %constant.12.clone.1) | dynamic-update-slice | bytes 262148 | tf_op jit(solution)/shard_map/dynamic_update_slice | solution.py:233
  218.8 4.4 %dynamic_update_slice.7 = bf16[16,65536]{1,0:T(8,128)(2,1)S(1)} dynamic-update-slice(bf16[16,65536]{1,0:T(8,128)(2,1)S(1)} %dynamic_update_slice.6, bf16[1,65536]{1,0:T(2,128)(2,1)S(1)} %get-tuple-element.44, s32[]{:T(128)S(6)} %select_n.62, s32[]{:T(128)} %constant.12.clone.1) | dynamic-update-slice | bytes 262148 | tf_op jit(solution)/shard_map/dynamic_update_slice | solution.py:233
  223.2 3.4 %convolution_convert_fusion.4 = bf16[16,3584]{1,0:T(8,128)(2,1)S(1)} fusion(bf16[512,3584]{1,0:T(8,128)(2,1)} %bitcast.21, bf16[16,256]{1,0:T(8,128)(2,1)S(1)} %get-tuple-element.42), kind=kOutput, calls=%fused_computation.11 | convolution fusion | flops 58810368 | bytes 3792896 | tf_op jit(solution)/shard_map/dot_general | solution.py:203
  226.6 33.4 %all-to-all-done.3 = bf16[64,8,3584]{2,1,0:T(8,128)(2,1)} async-done(((bf16[64,8,3584]{2,1,0:T(8,128)(2,1)}), bf16[64,8,3584]{2,1,0:T(8,128)(2,1)}, u32[]{:S(2)}, u32[]{:S(2)}) %all-to-all-start.3) | async-done | bytes 3670048 | tf_op jit(solution)/shard_map/all_to_all | solution.py:199
  260.0 2.6 convolution_convert_fusion.3
  262.6 0.7 pad_maximum_fusion
  (43 shorter events, 0.2 us)
Async XLA Ops:
  2.9 6.7 %collective-permute-start = (bf16[2,7168]{1,0:T(2,128)(2,1)S(1)}, bf16[2,7168]{1,0:T(2,128)(2,1)S(1)}, u32[]{:S(2)}, u32[]{:S(2)}) collective-permute-start(bf16[2,7168]{1,0:T(2,128)(2,1)S(1)} %gather_fusion), channel_id=1, source_target_pairs={{0,32},{32,0},{1,33},{33,1},{2,34},{34,2},{3,35},{35,3},{4,36},{36... | collective-permute-start | bytes 86024 | tf_op jit(solution)/shard_map/ppermute | solution.py:23
  3.0 6.6 %collective-permute-start.1 = (bf16[2,7168]{1,0:T(2,128)(2,1)S(1)}, bf16[2,7168]{1,0:T(2,128)(2,1)S(1)}, u32[]{:S(2)}, u32[]{:S(2)}) collective-permute-start(bf16[2,7168]{1,0:T(2,128)(2,1)S(1)} %gather_fusion), channel_id=1, source_target_pairs={{0,64},{64,0},{1,65},{65,1},{2,66},{66,2},{3,67},{67,3},{4,68},{68... | collective-permute-start | bytes 86024 | tf_op jit(solution)/shard_map/ppermute | solution.py:23
  3.8 5.8 %collective-permute-start.2 = (bf16[2,7168]{1,0:T(2,128)(2,1)S(1)}, bf16[2,7168]{1,0:T(2,128)(2,1)S(1)}, u32[]{:S(2)}, u32[]{:S(2)}) collective-permute-start(bf16[2,7168]{1,0:T(2,128)(2,1)S(1)} %gather_fusion), channel_id=1, source_target_pairs={{0,96},{32,64},{64,32},{96,0},{1,97},{33,65},{65,33},{97,1},{2,98}... | collective-permute-start | bytes 86024 | tf_op jit(solution)/shard_map/ppermute | solution.py:23
  13.6 58.4 %all-to-all-start = ((bf16[64,8,3584]{2,1,0:T(8,128)(2,1)}), bf16[64,8,3584]{2,1,0:T(8,128)(2,1)}, u32[]{:S(2)}, u32[]{:S(2)}) async-start(bf16[64,8,3584]{2,1,0:T(8,128)(2,1)} %bitcast.54), calls=%async_computation | async-start | bytes 7340032 | tf_op jit(solution)/shard_map/all_to_all | solution.py:199
  24.7 3.6 %copy-start.6 = (s32[1,2]{1,0:T(1,128)S(1)}, s32[1,2]{1,0:T(1,128)}, u32[]{:S(2)}) copy-start(s32[1,2]{1,0:T(1,128)} %param.17) | copy-start | bytes 28
  24.7 8.0 %copy-start.8 = (s32[1,128]{1,0:T(1,128)S(1)}, s32[1,128]{1,0:T(1,128)}, u32[]{:S(2)}) copy-start(s32[1,128]{1,0:T(1,128)} %param.16) | copy-start | bytes 1540
  24.7 8.1 %copy-start.7 = (s32[1,16]{1,0:T(1,128)S(1)}, s32[1,16]{1,0:T(1,128)}, u32[]{:S(2)}) copy-start(s32[1,16]{1,0:T(1,128)} %param.15) | copy-start | bytes 196
  24.7 81.9 %collective-permute-start.4 = (bf16[7168,256]{1,0:T(8,128)(2,1)}, bf16[7168,256]{1,0:T(8,128)(2,1)}, u32[]{:S(2)}, u32[]{:S(2)}) collective-permute-start(bf16[7168,256]{1,0:T(8,128)(2,1)} %bitcast.70), channel_id=1, source_target_pairs={{0,32},{32,0},{1,33},{33,1},{2,34},{34,2},{3,35},{35,3},{4,36},{36... | collective-permute-start | bytes 11010056 | tf_op jit(solution)/shard_map/ppermute | solution.py:23
  24.8 86.3 %collective-permute-start.3 = (bf16[7168,256]{1,0:T(8,128)(2,1)}, bf16[7168,256]{1,0:T(8,128)(2,1)}, u32[]{:S(2)}, u32[]{:S(2)}) collective-permute-start(bf16[7168,256]{1,0:T(8,128)(2,1)} %bitcast.68), channel_id=1, source_target_pairs={{0,32},{32,0},{1,33},{33,1},{2,34},{34,2},{3,35},{35,3},{4,36},{36... | collective-permute-start | bytes 11010056 | tf_op jit(solution)/shard_map/ppermute | solution.py:23
  25.3 78.5 %collective-permute-start.5 = (bf16[256,7168]{1,0:T(8,128)(2,1)}, bf16[256,7168]{1,0:T(8,128)(2,1)}, u32[]{:S(2)}, u32[]{:S(2)}) collective-permute-start(bf16[256,7168]{1,0:T(8,128)(2,1)} %bitcast.63), channel_id=1, source_target_pairs={{0,32},{32,0},{1,33},{33,1},{2,34},{34,2},{3,35},{35,3},{4,36},{36... | collective-permute-start | bytes 11010056 | tf_op jit(solution)/shard_map/ppermute | solution.py:23
  57.4 5.8 %copy-start = (bf16[128,32,1152]{2,1,0:T(8,128)(2,1)S(1)}, bf16[128,32,1152]{2,1,0:T(8,128)(2,1)}, u32[]{:S(2)}) copy-start(bf16[128,32,1152]{2,1,0:T(8,128)(2,1)} %gather_fusion.1) | copy-start | bytes 28311556
  63.1 3.0 %copy-start.5 = (bf16[16,7168]{1,0:T(8,128)(2,1)S(1)}, bf16[16,7168]{1,0:T(8,128)(2,1)}, u32[]{:S(2)}) copy-start(bf16[16,7168]{1,0:T(8,128)(2,1)} %param.14) | copy-start | bytes 688132
  72.0 10.4 %copy-start.3 = (f32[16,128,256]{2,1,0:T(8,128)S(1)}, f32[16,128,256]{2,1,0:T(8,128)}, u32[]{:S(2)}) copy-start(f32[16,128,256]{2,1,0:T(8,128)} %get-tuple-element.53) | copy-start | bytes 6291460
  72.0 57.2 %all-to-all-start.1 = ((bf16[64,8,3584]{2,1,0:T(8,128)(2,1)}), bf16[64,8,3584]{2,1,0:T(8,128)(2,1)}, u32[]{:S(2)}, u32[]{:S(2)}) async-start(bf16[64,8,3584]{2,1,0:T(8,128)(2,1)} %bitcast.55), calls=%async_computation.1 | async-start | bytes 7340032 | tf_op jit(solution)/shard_map/all_to_all | solution.py:199
  82.4 3.2 %copy-start.4 = (f32[16,128,256]{2,1,0:T(8,128)S(1)}, f32[16,128,256]{2,1,0:T(8,128)}, u32[]{:S(2)}) copy-start(f32[16,128,256]{2,1,0:T(8,128)} %get-tuple-element.55) | copy-start | bytes 6291460
  95.1 4.7 %copy-start.2 = (bf16[1,7168,256]{2,1,0:T(8,128)(2,1)S(1)}, bf16[1,7168,256]{2,1,0:T(8,128)(2,1)}, u32[]{:S(2)}) copy-start(bf16[1,7168,256]{2,1,0:T(8,128)(2,1)} %param.21) | copy-start | bytes 11010052
  129.2 33.4 %collective-permute-start.6 = (bf16[2,65536]{1,0:T(2,128)(2,1)S(1)}, bf16[2,65536]{1,0:T(2,128)(2,1)S(1)}, u32[]{:S(2)}, u32[]{:S(2)}) collective-permute-start(bf16[2,65536]{1,0:T(2,128)(2,1)S(1)} %gather_fusion.2), channel_id=1, source_target_pairs={{0,32},{32,0},{1,33},{33,1},{2,34},{34,2},{3,35},{35,3},{4,36},{36... | collective-permute-start | bytes 786440 | tf_op jit(solution)/shard_map/ppermute | solution.py:23
  129.2 33.4 %collective-permute-start.7 = (bf16[2,65536]{1,0:T(2,128)(2,1)S(1)}, bf16[2,65536]{1,0:T(2,128)(2,1)S(1)}, u32[]{:S(2)}, u32[]{:S(2)}) collective-permute-start(bf16[2,65536]{1,0:T(2,128)(2,1)S(1)} %gather_fusion.2), channel_id=1, source_target_pairs={{0,64},{64,0},{1,65},{65,1},{2,66},{66,2},{3,67},{67,3},{4,68},{68... | collective-permute-start | bytes 786440 | tf_op jit(solution)/shard_map/ppermute | solution.py:23
  129.9 32.7 %collective-permute-start.8 = (bf16[2,65536]{1,0:T(2,128)(2,1)S(1)}, bf16[2,65536]{1,0:T(2,128)(2,1)S(1)}, u32[]{:S(2)}, u32[]{:S(2)}) collective-permute-start(bf16[2,65536]{1,0:T(2,128)(2,1)S(1)} %gather_fusion.2), channel_id=1, source_target_pairs={{0,96},{32,64},{64,32},{96,0},{1,97},{33,65},{65,33},{97,1},{2,98}... | collective-permute-start | bytes 786440 | tf_op jit(solution)/shard_map/ppermute | solution.py:23
  145.3 58.7 %all-to-all-start.2 = ((bf16[64,8,3584]{2,1,0:T(8,128)(2,1)}), bf16[64,8,3584]{2,1,0:T(8,128)(2,1)}, u32[]{:S(2)}, u32[]{:S(2)}) async-start(bf16[64,8,3584]{2,1,0:T(8,128)(2,1)} %bitcast.67), calls=%async_computation.2 | async-start | bytes 7340032 | tf_op jit(solution)/shard_map/all_to_all | solution.py:199
  204.1 55.9 %all-to-all-start.3 = ((bf16[64,8,3584]{2,1,0:T(8,128)(2,1)}), bf16[64,8,3584]{2,1,0:T(8,128)(2,1)}, u32[]{:S(2)}, u32[]{:S(2)}) async-start(bf16[64,8,3584]{2,1,0:T(8,128)(2,1)} %bitcast.66), calls=%async_computation.3 | async-start | bytes 7340032 | tf_op jit(solution)/shard_map/all_to_all | solution.py:199
  223.2 39.4 %copy-start.1 = (bf16[16,65536]{1,0:T(8,128)(2,1)}, bf16[16,65536]{1,0:T(8,128)(2,1)S(1)}, u32[]{:S(2)}) copy-start(bf16[16,65536]{1,0:T(8,128)(2,1)S(1)} %dynamic_update_slice.7) | copy-start | bytes 6291460

commit v3 on v2

--- a/solution.py
+++ b/solution.py
@@ -7,16 +7,20 @@
 
 HEADS = 128
 ROPE = 64
-TOP = 8
-OUT_A = 3584
-BACK_A = 3584
-STEP = 896
+EXPERTS = 32
+CAP = 8
+SIDE = 4
+PART_A = 3584
+LISTS = 128
+STEP = 1792
+TAIL_STEP = 896
 
 score_scale = 192.0 ** (-0.5)
 gain_step = 0.0625
 
 ALL = ("yl", "core", "x", "yh", "z")
-PEERS = ("yl", "x", "yh", "z")
+Y = ("yl", "yh")
+PLANE = ("x", "z")
 
 
 def flip(value, axes, mask):
@@ -31,9 +35,28 @@
     return jnp.where(which == 1, by_one, jnp.where(which == 2, by_two, by_three))
 
 
-def pairs_of(latent_pool, page_table, row_count, kv_width):
-    pages = latent_pool.reshape(latent_pool.shape[0], -1, 2 * kv_width)
-    return pages[page_table.reshape(-1)].reshape(row_count, -1, 2 * kv_width)
+def shift(value, axis, by):
+    index = (0, 2, 1, 3) if axis == Y else (0, 1, 2, 3)
+    return lax.ppermute(value, axis, [(index[i], index[(i + by) % SIDE]) for i in range(SIDE)])
+
+
+def gather(value, axis):
+    return jnp.stack([value] + [shift(value, axis, s) for s in range(1, SIDE)])
+
+
+def scatter_sum(blocks, axis):
+    total = blocks[0].astype(jnp.float32)
+    for s in range(1, SIDE):
+        total = total + shift(blocks[s], axis, SIDE - s).astype(jnp.float32)
+    return total
+
+
+def product(a, b):
+    return jnp.dot(a, b, preferred_element_type=jnp.float32)
+
+
+def pairs_of(latent_pool, kv_width):
+    return latent_pool.reshape(latent_pool.shape[0], -1, 2 * kv_width)
 
 
 def halves(pairs, kv_width):
@@ -109,7 +132,7 @@
 def finish(come, gates, ups, shares, downs, first, columns):
     places, rest = come.shape
     units = gates[0].shape[1]
-    steps, tail = rest // STEP, columns // STEP
+    steps, tail = rest // STEP, columns // TAIL_STEP
 
     def kernel(*refs):
         x, *refs = refs
@@ -121,7 +144,7 @@
         (STEP, units), lambda i: (first // STEP + jnp.minimum(i, steps - 1), 0)
     )
     share = pl.BlockSpec((places, units), lambda i: (0, 0))
-    down = pl.BlockSpec((units, STEP), lambda i: (0, jnp.maximum(i - steps, 0)))
+    down = pl.BlockSpec((units, TAIL_STEP), lambda i: (0, jnp.maximum(i - steps, 0)))
     work = 2 * places * 2 * units
     return pl.pallas_call(
         kernel,
@@ -131,7 +154,7 @@
         + [share] * 4
         + [down] * 2,
         out_specs=[
-            pl.BlockSpec((places, STEP), lambda i: (0, jnp.maximum(i - steps, 0))),
+            pl.BlockSpec((places, TAIL_STEP), lambda i: (0, jnp.maximum(i - steps, 0))),
             pl.BlockSpec((places, 2 * units), lambda i: (0, 0)),
         ],
         out_shape=[
@@ -148,6 +171,10 @@
     )(come, *gates, *ups, *shares, *downs)
 
 
+def exchange(blocks):
+    return lax.all_to_all(blocks, PLANE, split_axis=0, concat_axis=0, tiled=True)
+
+
 def body(
     latent_pool,
     queries,
@@ -162,77 +189,137 @@
     w_up,
     w_down,
 ):
-    experts = 32
-    row_count = queries.shape[0]
-    model_width = hidden.shape[1]
+    row_count, model_width = hidden.shape
+    part_b = model_width - PART_A
+    kv_width = queries.shape[1] // HEADS
     out_slots = send_slot.reshape(-1)
     flips = match.reshape(-1)
+    at_y = lax.axis_index("yh") * 2 + lax.axis_index("yl")
 
     arriving = swapped(hidden[out_slots], flips)
     slots = jnp.arange(row_count, dtype=jnp.int32)
-    leaving = (slots[:, None] == out_slots[None, :]).astype(jnp.float32)
-    staying = 1.0 - jnp.sum(leaving, axis=1)
-
-    capacity = min(row_count, max(2, 2 * row_count * TOP // experts))
-    expert_ids = jnp.arange(experts, dtype=jnp.int32)
-    named = (routes[:, :, None] == expert_ids).astype(jnp.int32)
+    token_rows = hidden
+    for k in range(out_slots.shape[0]):
+        token_rows = jnp.where((slots == out_slots[k])[:, None], arriving[k], token_rows)
+
+    named = (routes[:, :, None] == jnp.arange(EXPERTS, dtype=jnp.int32)).astype(jnp.int32)
     chosen = jnp.sum(named, axis=1)
-    rank = jnp.cumsum(chosen, axis=0) - chosen
-    gain_of = jnp.sum(named * route_gain[:, :, None], axis=1).astype(jnp.float32) * gain_step
-    at_slot = (rank[:, :, None] == jnp.arange(capacity, dtype=jnp.int32)) & (chosen[:, :, None] > 0)
-    table = at_slot.astype(jnp.float32).reshape(row_count, experts * capacity)
-    gain_table = jnp.where(at_slot, gain_of[:, :, None], 0.0).reshape(row_count, experts * capacity)
-
-    places = 2 * experts * capacity
-    picks = jnp.concatenate([table * staying[:, None], jnp.dot(leaving.T, table)], axis=0)
-    picks = jnp.concatenate([picks, picks], axis=1).astype(jnp.bfloat16)
-    rows = jnp.concatenate([hidden, arriving], axis=0)
-
-    def leave(cut):
-        out = lax.dot_general(
-            picks, cut, (((0,), (0,)), ((), ())), preferred_element_type=jnp.float32
-        )
-        return out.astype(jnp.bfloat16)
-
-    def exchange(blocks):
-        blocks = blocks.reshape(2 * experts, capacity, -1)
-        out = lax.all_to_all(blocks, PEERS, split_axis=0, concat_axis=0, tiled=True)
-        return out.reshape(places, -1)
-
-    def product(a, b):
-        return jnp.dot(a, b, preferred_element_type=jnp.float32)
-
-    gates = (w_gate[0], flip(w_gate[0], ("core",), 1))
-    ups = (w_up[0], flip(w_up[0], ("core",), 1))
-    downs = (w_down[0], flip(w_down[0], ("core",), 1))
-    mix = jnp.concatenate([gain_table, gain_table], axis=1).astype(jnp.bfloat16)
-
-    kv_width = queries.shape[1] // HEADS
-    leave_a = leave(rows[:, :OUT_A])
-    leave_a, latent_pool, queries = lax.optimization_barrier((leave_a, latent_pool, queries))
-    come_a = exchange(leave_a)
-    leave_b = leave(rows[:, OUT_A:])
-    pairs = pairs_of(latent_pool, page_table, row_count, kv_width)
+    place = jnp.cumsum(chosen, axis=0) * chosen
+    gain = jnp.sum(named * route_gain[:, :, None], axis=1)
+    lists = jnp.concatenate(
+        [place, gain, jnp.zeros((row_count, LISTS - 2 * EXPERTS), jnp.int32)], axis=1
+    ).astype(jnp.bfloat16)
+
+    send_b = jnp.concatenate([token_rows[:, PART_A:], lists], axis=1)
+    send_b = jnp.broadcast_to(send_b, (SIDE * SIDE,) + send_b.shape)
+    gate_other = flip(w_gate[0], ("core",), 1)
+    up_other = flip(w_up[0], ("core",), 1)
+    send_b, gate_other, up_other = lax.optimization_barrier((send_b, gate_other, up_other))
+    rows_b = exchange(send_b)
+    rows_a = gather(jnp.concatenate([token_rows[:, :PART_A], lists], axis=1), Y)
+    rows_a = rows_a.reshape(SIDE * row_count, PART_A + LISTS)
+    rows_a, latent_pool = lax.optimization_barrier((rows_a, latent_pool))
+    pages = pairs_of(latent_pool, kv_width)
+    down_other = flip(w_down[0], ("core",), 1)
+
+    def listed(rows, width, yh):
+        lists = rows[:, width:].astype(jnp.float32)
+        out = []
+        for c in range(2):
+            cut = lists[:, c * EXPERTS : (c + 1) * EXPERTS].reshape(-1, SIDE, 2, SIDE)
+            out.append(jnp.where(yh == 0, cut[:, :, 0], cut[:, :, 1]))
+        return out
+
+    numbers = jnp.arange(1, CAP + 1, dtype=jnp.float32)
+
+    place_a, gain_a = listed(rows_a, PART_A, lax.axis_index("yh"))
+    source = jnp.arange(SIDE * row_count, dtype=jnp.int32) // row_count
+    own = source[:, None] == jnp.arange(SIDE, dtype=jnp.int32)
+    hit_a = (place_a[:, :, :, None, None] == numbers) & own[:, None, None, :, None]
+    hit_a = hit_a.reshape(SIDE * row_count, -1)
+    weight_a = jnp.broadcast_to(
+        gain_a[:, :, :, None], (SIDE * row_count, SIDE, SIDE, SIDE * CAP)
+    ).reshape(SIDE * row_count, -1)
+    mix_a = jnp.where(hit_a, weight_a * gain_step, 0.0).astype(jnp.bfloat16)
+    send_a = lax.dot_general(
+        hit_a.astype(jnp.bfloat16),
+        rows_a[:, :PART_A],
+        (((0,), (0,)), ((), ())),
+        preferred_element_type=jnp.float32,
+    ).astype(jnp.bfloat16)
+    send_a = send_a.reshape(SIDE * SIDE, SIDE * CAP, PART_A)
+    send_a, rows_b, pages, queries, down_other = lax.optimization_barrier(
+        (send_a, rows_b, pages, queries, down_other)
+    )
+    come_a = exchange(send_a).reshape(-1, PART_A)
+
+    rows_b = rows_b.reshape(-1, part_b + LISTS)
+    source = jnp.arange(SIDE * SIDE * row_count, dtype=jnp.int32) // row_count
+    here = source[:, None] == jnp.arange(SIDE * SIDE, dtype=jnp.int32)
+    sides = jnp.arange(SIDE, dtype=jnp.int32)
+    at_column = (sides[:, None] == lax.axis_index("x")) & (sides == lax.axis_index("z"))
+    both = []
+    for yh in range(2):
+        place_b, gain_b = listed(rows_b, part_b, yh)
+        place_b = jnp.sum(jnp.where(at_column, place_b, 0.0), axis=(1, 2))
+        gain_b = jnp.sum(jnp.where(at_column, gain_b, 0.0), axis=(1, 2))
+        hit = here[:, :, None] & (place_b[:, None, None] == numbers)
+        hit = hit.reshape(source.shape[0], -1)
+        both.append((hit, jnp.where(hit, gain_b[:, None] * gain_step, 0.0)))
+    columns_b, mixes_b = [], []
+    for k in range(SIDE):
+        low = (at_y + k) % SIDE < 2
+        columns_b.append(jnp.where(low, both[0][0], both[1][0]).astype(jnp.bfloat16))
+        mixes_b.append(jnp.where(low, both[0][1], both[1][1]).astype(jnp.bfloat16))
+    come_b = []
+    for k in (1, 3, 2, 0):
+        block = lax.dot_general(
+            columns_b[k],
+            rows_b[:, :part_b],
+            (((0,), (0,)), ((), ())),
+            preferred_element_type=jnp.float32,
+        ).astype(jnp.bfloat16)
+        come_b.append(block if k == 0 else shift(block, Y, k))
+    come_b = [come_b[i] for i in (3, 0, 2, 1)]
+    come_b = jnp.stack([block.reshape(SIDE * SIDE, CAP, part_b) for block in come_b], axis=1)
+    come_b = come_b.reshape(-1, part_b)
+
+    gates, ups, downs = (w_gate[0], gate_other), (w_up[0], up_other), (w_down[0], down_other)
+    joined = jnp.concatenate([w[:, PART_A:] for w in downs], axis=0)
+    shares = [product(come_b, w[PART_A:]) for w in gates + ups]
+
+    pairs = pages[page_table.reshape(-1)].reshape(row_count, -1, 2 * kv_width)
     query_heads = queries.reshape(row_count, HEADS, kv_width)
-    come_a, leave_b = lax.optimization_barrier((come_a, leave_b))
-    come_b = exchange(leave_b)
-    shares = [product(come_a, w[:OUT_A]) for w in gates + ups]
+    come_a, shares, joined, pairs, query_heads = lax.optimization_barrier(
+        (come_a, shares, joined, pairs, query_heads)
+    )
+    back_a, activated = finish(come_a, gates, ups, shares, downs, 0, PART_A)
+    back_a, activated, pairs, query_heads = lax.optimization_barrier(
+        (back_a, activated, pairs, query_heads)
+    )
+
+    final_a = exchange(back_a.reshape(SIDE * SIDE, SIDE * CAP, PART_A)).reshape(-1, PART_A)
+
+    by_source = activated.reshape(SIDE * SIDE, SIDE, CAP, -1)
+    final_b = []
+    for s in (1, 3, 2, 0):
+        block = by_source[:, s].reshape(SIDE * SIDE * CAP, -1)
+        block = product(block, joined).astype(jnp.bfloat16)
+        final_b.append(block if s == 0 else shift(block, Y, SIDE - s))
+    final_b = jnp.concatenate([final_b[i] for i in (3, 0, 2, 1)], axis=0)
+    mix_b = jnp.concatenate(mixes_b, axis=1)
+    moe_b = product(mix_b, final_b).astype(jnp.bfloat16)
+    moe_b = moe_b.reshape(SIDE * SIDE, row_count, part_b)
     probs = probabilities(pairs, query_heads, lengths)
     context = contexts(probs, pairs, kv_width)
-    moving = context[out_slots]
-    come_b, shares, context, moving = lax.optimization_barrier((come_b, shares, context, moving))
-    back_a, activated = finish(come_b, gates, ups, shares, downs, OUT_A, BACK_A)
-    back_a, activated = lax.optimization_barrier((back_a, activated))
-    final_a = exchange(back_a)
-    joined = jnp.concatenate([w[:, BACK_A:] for w in downs], axis=0)
-    back_b = product(activated, joined).astype(jnp.bfloat16)
-    back = swapped(moving, flips)
-    final_a, back_b, context, back = lax.optimization_barrier((final_a, back_b, context, back))
-    final_b = exchange(back_b)
+    final_a, moe_b, context = lax.optimization_barrier((final_a, moe_b, context))
+    moe_b = jnp.sum(exchange(moe_b).astype(jnp.float32), axis=0).astype(jnp.bfloat16)
+    moe_a = product(mix_a, final_a).astype(jnp.bfloat16)
+    moe_a = scatter_sum(moe_a.reshape(SIDE, row_count, PART_A), Y).astype(jnp.bfloat16)
+    moe_a, context = lax.optimization_barrier((moe_a, context))
+    back = swapped(context[out_slots], flips)
     for k in range(out_slots.shape[0]):
         context = lax.dynamic_update_slice_in_dim(context, back[k : k + 1], out_slots[k], 0)
-    moe_a = product(mix, final_a).astype(jnp.bfloat16)
-    moe_b = product(mix, final_b).astype(jnp.bfloat16)
     return (context, jnp.concatenate([moe_a, moe_b], axis=1))
 
 

time: 266 us -> 250 us (0.940)
  the two profiles are of different devices: /device:TPU:58 before, /device:TPU:0 now
where the time goes in v3:
time: 250 us; the launch traced here: 249 us
  waiting for transfers between devices  68.9 us (28%)
  local copies, waits for them, and re-layouts  51.4 us (21%)
  starting transfers between devices  46.8 us (19%)
  matrix products  44.5 us (18%)
  other arithmetic  17.9 us (7%)
  Pallas kernels  14 us (6%)
  between operations  4.92 us (2%)
    all_to_all x4, waiting for transfers between devices, exchange(): lax.all_to_all(blocks, PLANE, split_axis=0, concat_axis=0, tiled=True)  37.8 us
    ppermute x12, waiting for transfers between devices, shift(): lax.ppermute(value, axis, [(index[i], index[(i + by) % SIDE]) for i in ra...  28.2 us
    all_to_all x4, starting transfers between devices, exchange(): lax.all_to_all(blocks, PLANE, split_axis=0, concat_axis=0, tiled=True)  24.4 us
    dot_general x10, matrix products, product(): return jnp.dot(a, b, preferred_element_type=jnp.float32)  24 us
    ppermute x12, starting transfers between devices, shift(): lax.ppermute(value, axis, [(index[i], index[(i + by) % SIDE]) for i in ra...  17.6 us
    unnamed x40, local copies, waits for them, and re-layouts  14 us
    pallas_call x1, Pallas kernels, finish(): pl.pallas_call(kernel, grid=(steps + tail,), in_specs=[pl.BlockSpec((plac...  14 us
    gather x1, local copies, waits for them, and re-layouts, body(): pairs = pages[page_table.reshape(-1)].reshape(row_count, -1, 2 * kv_width)  11 us
  transfers between devices with their start and end apart: 25, of which 11 were waited for; matrix products, arithmetic and copies ran while one was open for 39% of the time, Pallas kernels for 0%

profile of v3, /device:TPU:0, one launch (start us, length us, event | category | flops | bytes accessed | tf_op | source)
XLA Modules:
  0.0 248.5 jit_solution(11696279886433370337)
XLA Ops:
  1.3 1.6 gather_fusion
  3.0 1.7 collective-permute-start.1
  5.3 1.3 fusion.110
  7.4 0.8 copy.43
  8.1 0.8 copy.44
  10.5 1.3 iota_compare_fusion.5
  12.5 1.0 select_select_fusion.4
  13.7 1.7 collective-permute-start.3
  15.4 2.9 %collective-permute-start.4 = (bf16[16,3712]{1,0:T(8,128)(2,1)S(1)}, bf16[16,3712]{1,0:T(8,128)(2,1)S(1)}, u32[]{:S(2)}, u32[]{:S(2)}) collective-permute-start(bf16[16,3712]{1,0:T(8,128)(2,1)S(1)} %concatenate.22), channel_id=1, source_target_pairs={{0,4},{64,68},{4,0},{68,64},{1,5},{65,69},{5,1},{69,65},{2,6},{66,... | collective-permute-start | bytes 356360 | tf_op jit(solution)/shard_map/ppermute | solution.py:40
  18.3 1.3 collective-permute-start.5
  19.6 2.9 %slice.220 = bf16[256,3584]{1,0:T(8,128)(2,1)} slice(bf16[256,7168]{1,0:T(8,128)(2,1)} %bitcast.175), slice={[0:256], [3584:7168]} | slice | bytes 3670016 | tf_op jit(solution)/shard_map/slice | solution.py:288
  22.6 1.4 broadcast_in_dim.150
  24.0 7.9 %all-to-all-start = ((bf16[16,16,3712]{2,1,0:T(8,128)(2,1)}), bf16[16,16,3712]{2,1,0:T(8,128)(2,1)S(1)}, u32[]{:S(2)}, u32[]{:S(2)}) async-start(bf16[16,16,3712]{2,1,0:T(8,128)(2,1)} %broadcast_in_dim.150), calls=%async_computation | async-start | bytes 3801088 | tf_op jit(solution)/shard_map/all_to_all | solution.py:175
  32.1 9.2 %copy.59 = bf16[16,8,32,1152]{3,2,1,0:T(8,128)(2,1)} copy(bf16[16,8,32,1152]{3,1,2,0:T(8,128)(2,1)} %bitcast.165) | data formatting | bytes 18874368
  42.2 3.0 %convolution_convert_fusion = bf16[512,3584]{1,0:T(8,128)(2,1)} fusion(pred[64,512]{0,1:T(8,128)(4,1)S(1)} %bitcast.191, bf16[64,3712]{1,0:T(8,128)(2,1)S(1)} %bitcast.188), kind=kOutput, calls=%fused_computation.3 | convolution fusion | flops 236716032 | bytes 4194304 | tf_op jit(solution)/shard_map/dot_general | solution.py:244
  45.2 13.7 %all-to-all-done = bf16[16,16,3712]{2,1,0:T(8,128)(2,1)S(1)} async-done(((bf16[16,16,3712]{2,1,0:T(8,128)(2,1)}), bf16[16,16,3712]{2,1,0:T(8,128)(2,1)S(1)}, u32[]{:S(2)}, u32[]{:S(2)}) %all-to-all-start) | async-done | bytes 1900576 | tf_op jit(solution)/shard_map/all_to_all | solution.py:175
  59.3 1.3 convolution_convert_fusion.8
  61.4 1.4 convolution_convert_fusion.7
  62.7 1.2 collective-permute-start.10
  63.9 1.4 convolution_convert_fusion.6
  65.3 1.5 collective-permute-start.11
  66.7 4.7 %all-to-all-start.1 = ((bf16[16,32,3584]{2,1,0:T(8,128)(2,1)}), bf16[16,32,3584]{2,1,0:T(8,128)(2,1)}, u32[]{:S(2)}, u32[]{:S(2)}) async-start(bf16[16,32,3584]{2,1,0:T(8,128)(2,1)} %bitcast.164), calls=%async_computation.1 | async-start | bytes 7340032 | tf_op jit(solution)/shard_map/all_to_all | solution.py:175
  71.5 2.8 %slice.179 = bf16[256,3584]{1,0:T(8,128)(2,1)} slice(bf16[256,7168]{1,0:T(8,128)(2,1)} %collective-permute-done.8.refs_10_), slice={[0:256], [3584:7168]} | slice | bytes 3670016 | tf_op jit(solution)/shard_map/slice | solution.py:288
  74.3 5.4 %reshape.448 = bf16[16,128,576]{2,1,0:T(8,128)(2,1)} reshape(bf16[16,73728]{1,0:T(8,128)(2,1)} %param.13) | data formatting | bytes 4718592 | tf_op jit(solution)/shard_map/reshape | solution.py:292
  79.7 11.0 %gather_fusion.1 = bf16[128,32,1152]{2,1,0:T(8,128)(2,1)} fusion(bf16[128,32,1152]{2,1,0:T(8,128)(2,1)} %bitcast.163, s32[1024]{0:T(1024)S(1)} %pad_clamp_fusion), kind=kCustom, calls=%fused_computation.1 | custom fusion | bytes 18874880 | tf_op jit(solution)/shard_map/gather | solution.py:291
  92.3 3.6 %pad_maximum_fusion.1 = bf16[512,3584]{1,0:T(8,128)(2,1)} fusion(bf16[256,3584]{1,0:T(8,128)(2,1)} %slice.179, bf16[256,3584]{1,0:T(8,128)(2,1)S(1)} %copy-done.3), kind=kLoop, calls=%fused_computation.25 | loop fusion | flops 7340032 | bytes 7340032 | tf_op jit(solution)/shard_map/concatenate | solution.py:288
  96.0 3.7 %collective-permute-done.9 = bf16[128,3584]{1,0:T(8,128)(2,1)S(1)} collective-permute-done((bf16[128,3584]{1,0:T(8,128)(2,1)}, bf16[128,3584]{1,0:T(8,128)(2,1)S(1)}, u32[]{:S(2)}, u32[]{:S(2)}) %collective-permute-start.9) | collective-permute-done | bytes 917536 | tf_op jit(solution)/shard_map/ppermute | solution.py:40
  99.7 2.1 collective-permute-done.11
  101.8 1.8 pad_maximum_fusion
  104.4 1.9 fusion.22.refs_7_
  106.4 1.9 fusion.24.refs_5_
  108.3 3.4 %fusion.26.refs_8_ = f32[512,256]{1,0:T(8,128)} fusion(bf16[512,3584]{1,0:T(8,128)(2,1)S(1)} %bitcast.180, bf16[7168,256]{1,0:T(8,128)(2,1)} %collective-permute-done.7.refs_4_), kind=kOutput, calls=%fused_computation.47 | convolution fusion | flops 939524096 | bytes 6029312 | tf_op jit(solution)/shard_map/dot_general | solution.py:55
  111.7 3.4 %fusion.29.refs_6_ = f32[512,256]{1,0:T(8,128)} fusion(bf16[512,3584]{1,0:T(8,128)(2,1)S(1)} %bitcast.181, bf16[7168,256]{1,0:T(8,128)(2,1)} %collective-permute-done.6.refs_2_), kind=kOutput, calls=%fused_computation.50 | convolution fusion | flops 939524096 | bytes 6029312 | tf_op jit(solution)/shard_map/dot_general | solution.py:55
  115.1 14.0 %shard_map.131 = (bf16[512,3584]{1,0:T(8,128)(2,1)}, bf16[512,512]{1,0:T(8,128)(2,1)}) custom-call(bf16[512,3584]{1,0:T(8,128)(2,1)} %bitcast.21.refs_0_, bf16[7168,256]{1,0:T(8,128)(2,1)} %bitcast.183, bf16[7168,256]{1,0:T(8,128)(2,1)} %collective-permute-done.6.refs_2_, bf16[7168,256]{1,0:T(8,128)(2,1)} %bitcast.185, ...), custom_call_target="tpu_custom_call" | custom-call | flops 5637144576 | bytes 18350080 | tf_op jit(solution)/shard_map/pallas_call | solution.py:149
  129.2 2.5 %convolution_convert_fusion.4 = bf16[128,3584]{1,0:T(8,128)(2,1)} fusion(bf16[512,3584]{1,0:T(8,128)(2,1)S(1)} %copy-done, bf16[16,4,8,512]{3,2,1,0:T(8,128)(2,1)} %bitcast.192), kind=kOutput, calls=%fused_computation.11 | convolution fusion | flops 470220800 | bytes 4718592 | tf_op jit(solution)/shard_map/dot_general | solution.py:55
  131.7 1.6 convolution_convert_fusion.3
  133.9 2.7 %collective-permute-start.12 = (bf16[128,3584]{1,0:T(8,128)(2,1)}, bf16[128,3584]{1,0:T(8,128)(2,1)}, u32[]{:S(2)}, u32[]{:S(2)}) collective-permute-start(bf16[128,3584]{1,0:T(8,128)(2,1)} %convolution_convert_fusion.4), channel_id=1, source_target_pairs={{0,68},{64,0},{4,64},{68,4},{1,69},{65,1},{5,65},{69,5},{2,70},{66... | collective-permute-start | bytes 2752520 | tf_op jit(solution)/shard_map/ppermute | solution.py:40
  136.6 0.9 collective-permute-start.14
  137.6 6.6 %all-to-all-start.2 = ((bf16[16,32,3584]{2,1,0:T(8,128)(2,1)}), bf16[16,32,3584]{2,1,0:T(8,128)(2,1)}, u32[]{:S(2)}, u32[]{:S(2)}) async-start(bf16[16,32,3584]{2,1,0:T(8,128)(2,1)} %bitcast.177), calls=%async_computation.2 | async-start | bytes 7340032 | tf_op jit(solution)/shard_map/all_to_all | solution.py:175
  144.2 4.3 %fusion.21 = (f32[16,128]{1,0:T(8,128)S(1)}, f32[16,128,256]{2,1,0:T(8,128)S(1)}) fusion(pred[16,256]{1,0:T(8,128)(4,1)S(1)} %get-tuple-element.87, bf16[16,256,1152]{2,1,0:T(8,128)(2,1)} %bitcast.166, bf16[16,128,576]{2,1,0:T(8,128)(2,1)S(1)} %copy-done.6), kind=kOutput, calls=%fused_computation.42 | convolution fusion | flops 672659456 | bytes 9711616 | tf_op jit(solution)/shard_map/rhc,rtc->rht/dot_general | solution.py:75
  148.6 4.5 %fusion.20 = (f32[16,128]{1,0:T(8,128)S(1)}, f32[16,128,256]{2,1,0:T(8,128)S(1)}) fusion(pred[16,256]{1,0:T(8,128)(4,1)S(1)} %get-tuple-element.88, bf16[16,256,1152]{2,1,0:T(8,128)(2,1)} %bitcast.167, bf16[16,128,576]{2,1,0:T(8,128)(2,1)S(1)} %copy-done.6), kind=kOutput, calls=%fused_computation.41 | convolution fusion | flops 672659456 | bytes 9711616 | tf_op jit(solution)/shard_map/rhc,rtc->rht/dot_general | solution.py:75
  153.1 2.2 fusion.33
  155.3 1.6 fusion.7
  157.0 2.6 %add_convert_fusion = bf16[16,128,512]{2,1,0:T(8,128)(2,1)S(1)} fusion(f32[16,128,512]{2,1,0:T(8,128)S(1)} %fusion.7, bf16[16,256,1152]{2,1,0:T(8,128)(2,1)S(1)} %bitcast.171, f32[16,128,256]{2,1,0:T(8,128)S(1)} %get-tuple-element.98, f32[16,128]{1,0:T(8,128)S(1)} %add.126, f32[16,128]{1,0:T(8,128)S(1)} %max.8, pred[16,256]{1,0:T(8,128)(4,1)S(1)} %get-tuple-element.87), kind=kOutput, calls=%fused_computation.21 | convolution fusion | flops 541589504 | bytes 12603392 | tf_op jit(solution)/shard_map/rht,rtc->rhc/dot_general | solution.py:96
  159.6 1.2 copy.60
  160.8 0.9 copy-done.1
  161.6 1.6 convolution_convert_fusion.5
  163.3 13.2 %collective-permute-done.12 = bf16[128,3584]{1,0:T(8,128)(2,1)} collective-permute-done((bf16[128,3584]{1,0:T(8,128)(2,1)}, bf16[128,3584]{1,0:T(8,128)(2,1)}, u32[]{:S(2)}, u32[]{:S(2)}) %collective-permute-start.12) | collective-permute-done | bytes 917536 | tf_op jit(solution)/shard_map/ppermute | solution.py:40
  176.4 3.2 %collective-permute-done.14 = bf16[128,3584]{1,0:T(8,128)(2,1)} collective-permute-done((bf16[128,3584]{1,0:T(8,128)(2,1)S(1)}, bf16[128,3584]{1,0:T(8,128)(2,1)}, u32[]{:S(2)}, u32[]{:S(2)}) %collective-permute-start.14) | collective-permute-done | bytes 917536 | tf_op jit(solution)/shard_map/ppermute | solution.py:40
  179.6 4.2 %convolution_convert_fusion.1 = bf16[256,3584]{1,0:T(8,128)(2,1)} fusion(bf16[128,3584]{1,0:T(8,128)(2,1)} %collective-permute-done.14, bf16[128,3584]{1,0:T(8,128)(2,1)} %collective-permute-done.13, bf16[128,3584]{1,0:T(8,128)(2,1)} %collective-permute-done.12, bf16[128,3584]{1,0:T(8,128)(2,1)S(1)} %convolution_convert_fusion.5, ...), kind=kOutput, calls=%fused_computation.8 | convolution fusion | flops 956170240 | bytes 5767168 | tf_op jit(solution)/shard_map/dot_general | solution.py:55
  183.8 8.5 %all-to-all-done.2 = bf16[16,32,3584]{2,1,0:T(8,128)(2,1)} async-done(((bf16[16,32,3584]{2,1,0:T(8,128)(2,1)}), bf16[16,32,3584]{2,1,0:T(8,128)(2,1)}, u32[]{:S(2)}, u32[]{:S(2)}) %all-to-all-start.2) | async-done | bytes 3670048 | tf_op jit(solution)/shard_map/all_to_all | solution.py:175
  192.3 2.8 %convolution_convert_fusion.10 = bf16[64,3584]{1,0:T(8,128)(2,1)S(1)} fusion(bf16[64,512]{0,1:T(8,128)(2,1)S(1)} %copy-done.8, bf16[512,3584]{1,0:T(8,128)(2,1)} %bitcast.42), kind=kOutput, calls=%fused_computation.18 | convolution fusion | flops 235110400 | bytes 4194304 | tf_op jit(solution)/shard_map/dot_general | solution.py:55
  195.2 2.6 %collective-permute-start.15 = (bf16[16,3584]{1,0:T(8,128)(2,1)S(1)}, bf16[16,3584]{1,0:T(8,128)(2,1)S(1)}, u32[]{:S(2)}, u32[]{:S(2)}) collective-permute-start(bf16[16,3584]{1,0:T(8,128)(2,1)S(1)} %get-tuple-element.72), channel_id=1, source_target_pairs={{0,68},{64,0},{4,64},{68,4},{1,69},{65,1},{5,65},{69,5},{2,70},{66... | collective-permute-start | bytes 344072 | tf_op jit(solution)/shard_map/ppermute | solution.py:40
  197.7 2.1 collective-permute-start.16
  200.5 3.5 %collective-permute-done.16 = bf16[16,3584]{1,0:T(8,128)(2,1)S(1)} collective-permute-done((bf16[16,3584]{1,0:T(8,128)(2,1)S(1)}, bf16[16,3584]{1,0:T(8,128)(2,1)S(1)}, u32[]{:S(2)}, u32[]{:S(2)}) %collective-permute-start.16) | collective-permute-done | bytes 114720 | tf_op jit(solution)/shard_map/ppermute | solution.py:40
  204.0 1.8 collective-permute-done.17
  205.9 0.9 gather_fusion.2
  207.0 1.7 collective-permute-start.20
  212.5 5.2 %all-to-all-start.3 = ((bf16[16,16,3584]{2,1,0:T(8,128)(2,1)}), bf16[16,16,3584]{2,1,0:T(8,128)(2,1)}, u32[]{:S(2)}, u32[]{:S(2)}) async-start(bf16[16,16,3584]{2,1,0:T(8,128)(2,1)} %bitcast.189), calls=%async_computation.3 | async-start | bytes 3670016 | tf_op jit(solution)/shard_map/all_to_all | solution.py:175
  217.7 3.0 %collective-permute-done.20 = bf16[2,65536]{1,0:T(2,128)(2,1)S(1)} collective-permute-done((bf16[2,65536]{1,0:T(2,128)(2,1)S(1)}, bf16[2,65536]{1,0:T(2,128)(2,1)S(1)}, u32[]{:S(2)}, u32[]{:S(2)}) %collective-permute-start.20) | collective-permute-done | bytes 262176 | tf_op jit(solution)/shard_map/ppermute | solution.py:27
  221.6 4.4 %dynamic_update_slice.6 = bf16[16,65536]{1,0:T(8,128)(2,1)S(1)} dynamic-update-slice(bf16[16,65536]{1,0:T(8,128)(2,1)S(1)} %bitcast.173, bf16[1,65536]{1,0:T(2,128)(2,1)S(1)} %get-tuple-element.76, s32[]{:T(128)S(6)} %select_n.235, s32[]{:T(128)} %constant.89.clone.1) | dynamic-update-slice | bytes 262148 | tf_op jit(solution)/shard_map/dynamic_update_slice | solution.py:322
  226.0 4.4 %dynamic_update_slice.7 = bf16[16,65536]{1,0:T(8,128)(2,1)S(1)} dynamic-update-slice(bf16[16,65536]{1,0:T(8,128)(2,1)S(1)} %dynamic_update_slice.6, bf16[1,65536]{1,0:T(2,128)(2,1)S(1)} %get-tuple-element.75, s32[]{:T(128)S(6)} %select_n.236, s32[]{:T(128)} %constant.89.clone.1) | dynamic-update-slice | bytes 262148 | tf_op jit(solution)/shard_map/dynamic_update_slice | solution.py:322
  230.4 15.6 %all-to-all-done.3 = bf16[16,16,3584]{2,1,0:T(8,128)(2,1)} async-done(((bf16[16,16,3584]{2,1,0:T(8,128)(2,1)}), bf16[16,16,3584]{2,1,0:T(8,128)(2,1)}, u32[]{:S(2)}, u32[]{:S(2)}) %all-to-all-start.3) | async-done | bytes 1835040 | tf_op jit(solution)/shard_map/all_to_all | solution.py:175
  246.1 1.7 reduce_sum.92
  (115 shorter events, 12.6 us)
Async XLA Ops:
  2.9 8.9 %collective-permute-start = (bf16[2,7168]{1,0:T(2,128)(2,1)S(1)}, bf16[2,7168]{1,0:T(2,128)(2,1)S(1)}, u32[]{:S(2)}, u32[]{:S(2)}) collective-permute-start(bf16[2,7168]{1,0:T(2,128)(2,1)S(1)} %gather_fusion), channel_id=1, source_target_pairs={{0,32},{32,0},{1,33},{33,1},{2,34},{34,2},{3,35},{35,3},{4,36},{36... | collective-permute-start | bytes 86024 | tf_op jit(solution)/shard_map/ppermute | solution.py:27
  3.0 9.3 %collective-permute-start.1 = (bf16[2,7168]{1,0:T(2,128)(2,1)S(1)}, bf16[2,7168]{1,0:T(2,128)(2,1)S(1)}, u32[]{:S(2)}, u32[]{:S(2)}) collective-permute-start(bf16[2,7168]{1,0:T(2,128)(2,1)S(1)} %gather_fusion), channel_id=1, source_target_pairs={{0,64},{64,0},{1,65},{65,1},{2,66},{66,2},{3,67},{67,3},{4,68},{68... | collective-permute-start | bytes 86024 | tf_op jit(solution)/shard_map/ppermute | solution.py:27
  4.7 7.5 %collective-permute-start.2 = (bf16[2,7168]{1,0:T(2,128)(2,1)S(1)}, bf16[2,7168]{1,0:T(2,128)(2,1)S(1)}, u32[]{:S(2)}, u32[]{:S(2)}) collective-permute-start(bf16[2,7168]{1,0:T(2,128)(2,1)S(1)} %gather_fusion), channel_id=1, source_target_pairs={{0,96},{32,64},{64,32},{96,0},{1,97},{33,65},{65,33},{97,1},{2,98}... | collective-permute-start | bytes 86024 | tf_op jit(solution)/shard_map/ppermute | solution.py:27
  4.8 13.4 %collective-permute-start.6 = (bf16[7168,256]{1,0:T(8,128)(2,1)}, bf16[7168,256]{1,0:T(8,128)(2,1)}, u32[]{:S(2)}, u32[]{:S(2)}) collective-permute-start(bf16[7168,256]{1,0:T(8,128)(2,1)} %bitcast.182), channel_id=1, source_target_pairs={{0,32},{32,0},{1,33},{33,1},{2,34},{34,2},{3,35},{35,3},{4,36},{36... | collective-permute-start | bytes 11010056 | tf_op jit(solution)/shard_map/ppermute | solution.py:27
  5.2 17.4 %collective-permute-start.7 = (bf16[7168,256]{1,0:T(8,128)(2,1)}, bf16[7168,256]{1,0:T(8,128)(2,1)}, u32[]{:S(2)}, u32[]{:S(2)}) collective-permute-start(bf16[7168,256]{1,0:T(8,128)(2,1)} %bitcast.184), channel_id=1, source_target_pairs={{0,32},{32,0},{1,33},{33,1},{2,34},{34,2},{3,35},{35,3},{4,36},{36... | collective-permute-start | bytes 11010056 | tf_op jit(solution)/shard_map/ppermute | solution.py:27
  7.3 15.1 %copy-start.13 = (pred[2]{0:T(512)(128)(4,1)}, pred[2]{0:T(512)(128)(4,1)S(1)}, u32[]{:S(2)}) copy-start(pred[2]{0:T(512)(128)(4,1)S(1)} %get-tuple-element.92) | copy-start | bytes 10
  11.8 33.4 %collective-permute-start.8 = (bf16[256,7168]{1,0:T(8,128)(2,1)}, bf16[256,7168]{1,0:T(8,128)(2,1)}, u32[]{:S(2)}, u32[]{:S(2)}) collective-permute-start(bf16[256,7168]{1,0:T(8,128)(2,1)} %bitcast.174), channel_id=1, source_target_pairs={{0,32},{32,0},{1,33},{33,1},{2,34},{34,2},{3,35},{35,3},{4,36},{36... | collective-permute-start | bytes 11010056 | tf_op jit(solution)/shard_map/ppermute | solution.py:27
  13.7 18.2 %collective-permute-start.3 = (bf16[16,3712]{1,0:T(8,128)(2,1)S(1)}, bf16[16,3712]{1,0:T(8,128)(2,1)S(1)}, u32[]{:S(2)}, u32[]{:S(2)}) collective-permute-start(bf16[16,3712]{1,0:T(8,128)(2,1)S(1)} %concatenate.22), channel_id=1, source_target_pairs={{0,64},{64,4},{4,68},{68,0},{1,65},{65,5},{5,69},{69,1},{2,66},{66... | collective-permute-start | bytes 356360 | tf_op jit(solution)/shard_map/ppermute | solution.py:40
  15.4 16.5 %collective-permute-start.4 = (bf16[16,3712]{1,0:T(8,128)(2,1)S(1)}, bf16[16,3712]{1,0:T(8,128)(2,1)S(1)}, u32[]{:S(2)}, u32[]{:S(2)}) collective-permute-start(bf16[16,3712]{1,0:T(8,128)(2,1)S(1)} %concatenate.22), channel_id=1, source_target_pairs={{0,4},{64,68},{4,0},{68,64},{1,5},{65,69},{5,1},{69,65},{2,6},{66,... | collective-permute-start | bytes 356360 | tf_op jit(solution)/shard_map/ppermute | solution.py:40
  18.3 13.6 %collective-permute-start.5 = (bf16[16,3712]{1,0:T(8,128)(2,1)S(1)}, bf16[16,3712]{1,0:T(8,128)(2,1)S(1)}, u32[]{:S(2)}, u32[]{:S(2)}) collective-permute-start(bf16[16,3712]{1,0:T(8,128)(2,1)S(1)} %concatenate.22), channel_id=1, source_target_pairs={{0,68},{64,0},{4,64},{68,4},{1,69},{65,1},{5,65},{69,5},{2,70},{66... | collective-permute-start | bytes 356360 | tf_op jit(solution)/shard_map/ppermute | solution.py:40
  24.0 34.9 %all-to-all-start = ((bf16[16,16,3712]{2,1,0:T(8,128)(2,1)}), bf16[16,16,3712]{2,1,0:T(8,128)(2,1)S(1)}, u32[]{:S(2)}, u32[]{:S(2)}) async-start(bf16[16,16,3712]{2,1,0:T(8,128)(2,1)} %broadcast_in_dim.150), calls=%async_computation | async-start | bytes 3801088 | tf_op jit(solution)/shard_map/all_to_all | solution.py:175
  60.7 39.0 %collective-permute-start.9 = (bf16[128,3584]{1,0:T(8,128)(2,1)}, bf16[128,3584]{1,0:T(8,128)(2,1)S(1)}, u32[]{:S(2)}, u32[]{:S(2)}) collective-permute-start(bf16[128,3584]{1,0:T(8,128)(2,1)} %convolution_convert_fusion.8), channel_id=1, source_target_pairs={{0,64},{64,4},{4,68},{68,0},{1,65},{65,5},{5,69},{69,1},{2,66},{66... | collective-permute-start | bytes 2752520 | tf_op jit(solution)/shard_map/ppermute | solution.py:40
  62.7 37.0 %collective-permute-start.10 = (bf16[128,3584]{1,0:T(8,128)(2,1)}, bf16[128,3584]{1,0:T(8,128)(2,1)}, u32[]{:S(2)}, u32[]{:S(2)}) collective-permute-start(bf16[128,3584]{1,0:T(8,128)(2,1)} %convolution_convert_fusion.7), channel_id=1, source_target_pairs={{0,4},{64,68},{4,0},{68,64},{1,5},{65,69},{5,1},{69,65},{2,6},{66,... | collective-permute-start | bytes 2752520 | tf_op jit(solution)/shard_map/ppermute | solution.py:40
  65.3 36.5 %collective-permute-start.11 = (bf16[128,3584]{1,0:T(8,128)(2,1)}, bf16[128,3584]{1,0:T(8,128)(2,1)}, u32[]{:S(2)}, u32[]{:S(2)}) collective-permute-start(bf16[128,3584]{1,0:T(8,128)(2,1)} %convolution_convert_fusion.6), channel_id=1, source_target_pairs={{0,68},{64,0},{4,64},{68,4},{1,69},{65,1},{5,65},{69,5},{2,70},{66... | collective-permute-start | bytes 2752520 | tf_op jit(solution)/shard_map/ppermute | solution.py:40
  66.7 48.4 %all-to-all-start.1 = ((bf16[16,32,3584]{2,1,0:T(8,128)(2,1)}), bf16[16,32,3584]{2,1,0:T(8,128)(2,1)}, u32[]{:S(2)}, u32[]{:S(2)}) async-start(bf16[16,32,3584]{2,1,0:T(8,128)(2,1)} %bitcast.164), calls=%async_computation.1 | async-start | bytes 7340032 | tf_op jit(solution)/shard_map/all_to_all | solution.py:175
  90.7 1.6 copy-start.3
  101.8 2.6 %copy-start.5 = (bf16[1,7168,256]{2,1,0:T(8,128)(2,1)S(1)}, bf16[1,7168,256]{2,1,0:T(8,128)(2,1)}, u32[]{:S(2)}) copy-start(bf16[1,7168,256]{2,1,0:T(8,128)(2,1)} %param.22) | copy-start | bytes 11010052
  104.4 2.0 copy-start.4
  115.1 14.0 %copy-start = (bf16[512,3584]{1,0:T(8,128)(2,1)S(1)}, bf16[512,3584]{1,0:T(8,128)(2,1)}, u32[]{:S(2)}) copy-start(bf16[512,3584]{1,0:T(8,128)(2,1)} %pad_maximum_fusion.1) | copy-start | bytes 11010052
  129.1 2.6 %copy-start.7 = (bf16[512,512]{1,0:T(8,128)(2,1)S(1)}, bf16[512,512]{1,0:T(8,128)(2,1)}, u32[]{:S(2)}) copy-start(bf16[512,512]{1,0:T(8,128)(2,1)} %get-tuple-element.51) | copy-start | bytes 1572868
  133.9 42.5 %collective-permute-start.12 = (bf16[128,3584]{1,0:T(8,128)(2,1)}, bf16[128,3584]{1,0:T(8,128)(2,1)}, u32[]{:S(2)}, u32[]{:S(2)}) collective-permute-start(bf16[128,3584]{1,0:T(8,128)(2,1)} %convolution_convert_fusion.4), channel_id=1, source_target_pairs={{0,68},{64,0},{4,64},{68,4},{1,69},{65,1},{5,65},{69,5},{2,70},{66... | collective-permute-start | bytes 2752520 | tf_op jit(solution)/shard_map/ppermute | solution.py:40
  136.6 39.8 %collective-permute-start.13 = (bf16[128,3584]{1,0:T(8,128)(2,1)}, bf16[128,3584]{1,0:T(8,128)(2,1)}, u32[]{:S(2)}, u32[]{:S(2)}) collective-permute-start(bf16[128,3584]{1,0:T(8,128)(2,1)} %convolution_convert_fusion.3), channel_id=1, source_target_pairs={{0,4},{64,68},{4,0},{68,64},{1,5},{65,69},{5,1},{69,65},{2,6},{66,... | collective-permute-start | bytes 2752520 | tf_op jit(solution)/shard_map/ppermute | solution.py:40
  136.6 43.0 %collective-permute-start.14 = (bf16[128,3584]{1,0:T(8,128)(2,1)S(1)}, bf16[128,3584]{1,0:T(8,128)(2,1)}, u32[]{:S(2)}, u32[]{:S(2)}) collective-permute-start(bf16[128,3584]{1,0:T(8,128)(2,1)S(1)} %convolution_convert_fusion.2), channel_id=1, source_target_pairs={{0,64},{64,4},{4,68},{68,0},{1,65},{65,5},{5,69},{69,1},{2,66},{66... | collective-permute-start | bytes 2752520 | tf_op jit(solution)/shard_map/ppermute | solution.py:40
  137.6 6.6 %copy-start.6 = (bf16[16,128,576]{2,1,0:T(8,128)(2,1)S(1)}, bf16[16,128,576]{2,1,0:T(8,128)(2,1)}, u32[]{:S(2)}) copy-start(bf16[16,128,576]{2,1,0:T(8,128)(2,1)} %reshape.448) | copy-start | bytes 7077892
  137.6 54.7 %all-to-all-start.2 = ((bf16[16,32,3584]{2,1,0:T(8,128)(2,1)}), bf16[16,32,3584]{2,1,0:T(8,128)(2,1)}, u32[]{:S(2)}, u32[]{:S(2)}) async-start(bf16[16,32,3584]{2,1,0:T(8,128)(2,1)} %bitcast.177), calls=%async_computation.2 | async-start | bytes 7340032 | tf_op jit(solution)/shard_map/all_to_all | solution.py:175
  144.2 11.1 %slice-start = ((s8[9437184]{0:T(1024)(128)(4,1)}), s8[4194304]{0:T(1024)(128)(4,1)S(1)}, s32[]{:S(2)}) async-start(s8[9437184]{0:T(1024)(128)(4,1)} %bitcast.168), calls=%async_computation.4 | async-start | bytes 8388608
  144.2 11.1 %slice-start.1 = ((s8[9437184]{0:T(1024)(128)(4,1)}), s8[4194304]{0:T(1024)(128)(4,1)S(1)}, s32[]{:S(2)}) async-start(s8[9437184]{0:T(1024)(128)(4,1)} %bitcast.168), calls=%async_computation.5 | async-start | bytes 8388608
  148.6 6.7 %slice-start.2 = ((s8[9437184]{0:T(1024)(128)(4,1)}), s8[1048576]{0:T(1024)(128)(4,1)S(1)}, s32[]{:S(2)}) async-start(s8[9437184]{0:T(1024)(128)(4,1)} %bitcast.168), calls=%async_computation.6 | async-start | bytes 2097152
  159.6 2.0 copy-start.1
  161.6 18.0 %copy-start.9 = (bf16[256,128]{0,1:T(8,128)(2,1)S(1)}, bf16[256,128]{0,1:T(8,128)(2,1)}, u32[]{:S(2)}) copy-start(bf16[256,128]{0,1:T(8,128)(2,1)} %get-tuple-element.83) | copy-start | bytes 196612
  161.6 18.0 %copy-start.10 = (bf16[256,128]{0,1:T(8,128)(2,1)S(1)}, bf16[256,128]{0,1:T(8,128)(2,1)}, u32[]{:S(2)}) copy-start(bf16[256,128]{0,1:T(8,128)(2,1)} %get-tuple-element.84) | copy-start | bytes 196612
  161.6 18.0 %copy-start.11 = (bf16[256,128]{0,1:T(8,128)(2,1)S(1)}, bf16[256,128]{0,1:T(8,128)(2,1)}, u32[]{:S(2)}) copy-start(bf16[256,128]{0,1:T(8,128)(2,1)} %get-tuple-element.85) | copy-start | bytes 196612
  161.6 18.0 %copy-start.12 = (bf16[256,128]{0,1:T(8,128)(2,1)S(1)}, bf16[256,128]{0,1:T(8,128)(2,1)}, u32[]{:S(2)}) copy-start(bf16[256,128]{0,1:T(8,128)(2,1)} %get-tuple-element.86) | copy-start | bytes 196612
  179.6 12.7 %copy-start.8 = (bf16[64,512]{0,1:T(8,128)(2,1)S(1)}, bf16[64,512]{0,1:T(8,128)(2,1)}, u32[]{:S(2)}) copy-start(bf16[64,512]{0,1:T(8,128)(2,1)} %fusion.56) | copy-start | bytes 196612
  195.2 5.4 %collective-permute-start.15 = (bf16[16,3584]{1,0:T(8,128)(2,1)S(1)}, bf16[16,3584]{1,0:T(8,128)(2,1)S(1)}, u32[]{:S(2)}, u32[]{:S(2)}) collective-permute-start(bf16[16,3584]{1,0:T(8,128)(2,1)S(1)} %get-tuple-element.72), channel_id=1, source_target_pairs={{0,68},{64,0},{4,64},{68,4},{1,69},{65,1},{5,65},{69,5},{2,70},{66... | collective-permute-start | bytes 344072 | tf_op jit(solution)/shard_map/ppermute | solution.py:40
  197.7 6.3 %collective-permute-start.16 = (bf16[16,3584]{1,0:T(8,128)(2,1)S(1)}, bf16[16,3584]{1,0:T(8,128)(2,1)S(1)}, u32[]{:S(2)}, u32[]{:S(2)}) collective-permute-start(bf16[16,3584]{1,0:T(8,128)(2,1)S(1)} %get-tuple-element.74), channel_id=1, source_target_pairs={{0,4},{64,68},{4,0},{68,64},{1,5},{65,69},{5,1},{69,65},{2,6},{66,... | collective-permute-start | bytes 344072 | tf_op jit(solution)/shard_map/ppermute | solution.py:40
  199.8 6.0 %collective-permute-start.17 = (bf16[16,3584]{1,0:T(8,128)(2,1)S(1)}, bf16[16,3584]{1,0:T(8,128)(2,1)S(1)}, u32[]{:S(2)}, u32[]{:S(2)}) collective-permute-start(bf16[16,3584]{1,0:T(8,128)(2,1)S(1)} %get-tuple-element.73), channel_id=1, source_target_pairs={{0,64},{64,4},{4,68},{68,0},{1,65},{65,5},{5,69},{69,1},{2,66},{66... | collective-permute-start | bytes 344072 | tf_op jit(solution)/shard_map/ppermute | solution.py:40
  205.9 14.9 %copy-start.14 = (pred[2]{0:T(512)(128)(4,1)S(1)}, pred[2]{0:T(512)(128)(4,1)}, u32[]{:S(2)}) copy-start(pred[2]{0:T(512)(128)(4,1)} %copy-done.13) | copy-start | bytes 10
  206.8 10.9 %collective-permute-start.18 = (bf16[2,65536]{1,0:T(2,128)(2,1)S(1)}, bf16[2,65536]{1,0:T(2,128)(2,1)S(1)}, u32[]{:S(2)}, u32[]{:S(2)}) collective-permute-start(bf16[2,65536]{1,0:T(2,128)(2,1)S(1)} %gather_fusion.2), channel_id=1, source_target_pairs={{0,32},{32,0},{1,33},{33,1},{2,34},{34,2},{3,35},{35,3},{4,36},{36... | collective-permute-start | bytes 786440 | tf_op jit(solution)/shard_map/ppermute | solution.py:27
  206.9 10.9 %collective-permute-start.19 = (bf16[2,65536]{1,0:T(2,128)(2,1)S(1)}, bf16[2,65536]{1,0:T(2,128)(2,1)S(1)}, u32[]{:S(2)}, u32[]{:S(2)}) collective-permute-start(bf16[2,65536]{1,0:T(2,128)(2,1)S(1)} %gather_fusion.2), channel_id=1, source_target_pairs={{0,64},{64,0},{1,65},{65,1},{2,66},{66,2},{3,67},{67,3},{4,68},{68... | collective-permute-start | bytes 786440 | tf_op jit(solution)/shard_map/ppermute | solution.py:27
  207.0 13.7 %collective-permute-start.20 = (bf16[2,65536]{1,0:T(2,128)(2,1)S(1)}, bf16[2,65536]{1,0:T(2,128)(2,1)S(1)}, u32[]{:S(2)}, u32[]{:S(2)}) collective-permute-start(bf16[2,65536]{1,0:T(2,128)(2,1)S(1)} %gather_fusion.2), channel_id=1, source_target_pairs={{0,96},{32,64},{64,32},{96,0},{1,97},{33,65},{65,33},{97,1},{2,98}... | collective-permute-start | bytes 786440 | tf_op jit(solution)/shard_map/ppermute | solution.py:27
  212.5 33.6 %all-to-all-start.3 = ((bf16[16,16,3584]{2,1,0:T(8,128)(2,1)}), bf16[16,16,3584]{2,1,0:T(8,128)(2,1)}, u32[]{:S(2)}, u32[]{:S(2)}) async-start(bf16[16,16,3584]{2,1,0:T(8,128)(2,1)} %bitcast.189), calls=%async_computation.3 | async-start | bytes 3670016 | tf_op jit(solution)/shard_map/all_to_all | solution.py:175
  230.4 18.1 %copy-start.2 = (bf16[16,65536]{1,0:T(8,128)(2,1)}, bf16[16,65536]{1,0:T(8,128)(2,1)S(1)}, u32[]{:S(2)}) copy-start(bf16[16,65536]{1,0:T(8,128)(2,1)S(1)} %dynamic_update_slice.7) | copy-start | bytes 6291460

commit v4 on v3

--- a/solution.py
+++ b/solution.py
@@ -316,7 +316,6 @@
     moe_b = jnp.sum(exchange(moe_b).astype(jnp.float32), axis=0).astype(jnp.bfloat16)
     moe_a = product(mix_a, final_a).astype(jnp.bfloat16)
     moe_a = scatter_sum(moe_a.reshape(SIDE, row_count, PART_A), Y).astype(jnp.bfloat16)
-    moe_a, context = lax.optimization_barrier((moe_a, context))
     back = swapped(context[out_slots], flips)
     for k in range(out_slots.shape[0]):
         context = lax.dynamic_update_slice_in_dim(context, back[k : k + 1], out_slots[k], 0)

time: 250 us -> 243 us (0.972)
  the two profiles are of different devices: /device:TPU:0 before, /device:TPU:16 now
where the time goes in v4:
time: 243 us; the launch traced here: 242 us
  waiting for transfers between devices  60.4 us (25%)
  local copies, waits for them, and re-layouts  52.7 us (22%)
  starting transfers between devices  46.6 us (19%)
  matrix products  44.5 us (18%)
  other arithmetic  18.9 us (8%)
  Pallas kernels  14 us (6%)
  between operations  4.92 us (2%)
    all_to_all x4, waiting for transfers between devices, exchange(): lax.all_to_all(blocks, PLANE, split_axis=0, concat_axis=0, tiled=True)  34.4 us
    dot_general x10, matrix products, product(): return jnp.dot(a, b, preferred_element_type=jnp.float32)  24 us
    all_to_all x4, starting transfers between devices, exchange(): lax.all_to_all(blocks, PLANE, split_axis=0, concat_axis=0, tiled=True)  23.9 us
    ppermute x12, waiting for transfers between devices, shift(): lax.ppermute(value, axis, [(index[i], index[(i + by) % SIDE]) for i in ra...  19.1 us
    ppermute x12, starting transfers between devices, shift(): lax.ppermute(value, axis, [(index[i], index[(i + by) % SIDE]) for i in ra...  16.9 us
    unnamed x42, local copies, waits for them, and re-layouts  14.6 us
    pallas_call x1, Pallas kernels, finish(): pl.pallas_call(kernel, grid=(steps + tail,), in_specs=[pl.BlockSpec((plac...  14 us
    gather x1, local copies, waits for them, and re-layouts, body(): pairs = pages[page_table.reshape(-1)].reshape(row_count, -1, 2 * kv_width)  11 us
  transfers between devices with their start and end apart: 25, of which 8 were waited for; matrix products, arithmetic and copies ran while one was open for 41% of the time, Pallas kernels for 0%

profile of v4, /device:TPU:16, one launch (start us, length us, event | category | flops | bytes accessed | tf_op | source)
XLA Modules:
  0.0 242.0 jit_solution(17092337068199979921)
XLA Ops:
  1.3 1.6 gather_fusion
  3.0 1.4 collective-permute-start.1
  5.3 1.3 fusion.110
  7.4 0.8 copy.43
  8.1 0.8 copy.44
  10.6 1.2 iota_compare_fusion.5
  12.5 1.0 select_select_fusion.4
  13.7 1.3 collective-permute-start.3
  15.6 1.0 collective-permute-start.5
  16.6 2.9 %slice.217 = bf16[256,3584]{1,0:T(8,128)(2,1)} slice(bf16[256,7168]{1,0:T(8,128)(2,1)} %bitcast.175), slice={[0:256], [3584:7168]} | slice | bytes 3670016 | tf_op jit(solution)/shard_map/slice | solution.py:288
  19.6 1.4 broadcast_in_dim.148
  21.0 8.0 %all-to-all-start = ((bf16[16,16,3712]{2,1,0:T(8,128)(2,1)}), bf16[16,16,3712]{2,1,0:T(8,128)(2,1)S(1)}, u32[]{:S(2)}, u32[]{:S(2)}) async-start(bf16[16,16,3712]{2,1,0:T(8,128)(2,1)} %broadcast_in_dim.148), calls=%async_computation | async-start | bytes 3801088 | tf_op jit(solution)/shard_map/all_to_all | solution.py:175
  29.2 9.2 %copy.59 = bf16[16,8,32,1152]{3,2,1,0:T(8,128)(2,1)} copy(bf16[16,8,32,1152]{3,1,2,0:T(8,128)(2,1)} %bitcast.165) | data formatting | bytes 18874368
  39.3 3.0 %convolution_convert_fusion = bf16[512,3584]{1,0:T(8,128)(2,1)} fusion(pred[64,512]{0,1:T(8,128)(4,1)S(1)} %bitcast.191, bf16[64,3712]{1,0:T(8,128)(2,1)S(1)} %bitcast.188), kind=kOutput, calls=%fused_computation.3 | convolution fusion | flops 236716032 | bytes 4194304 | tf_op jit(solution)/shard_map/dot_general | solution.py:244
  42.3 13.8 %all-to-all-done = bf16[16,16,3712]{2,1,0:T(8,128)(2,1)S(1)} async-done(((bf16[16,16,3712]{2,1,0:T(8,128)(2,1)}), bf16[16,16,3712]{2,1,0:T(8,128)(2,1)S(1)}, u32[]{:S(2)}, u32[]{:S(2)}) %all-to-all-start) | async-done | bytes 1900576 | tf_op jit(solution)/shard_map/all_to_all | solution.py:175
  56.6 1.4 convolution_convert_fusion.8
  57.9 1.4 collective-permute-start.9
  59.3 1.3 convolution_convert_fusion.7
  60.7 2.3 collective-permute-start.10
  63.0 1.4 convolution_convert_fusion.6
  64.3 2.0 collective-permute-start.11
  66.3 4.7 %all-to-all-start.1 = ((bf16[16,32,3584]{2,1,0:T(8,128)(2,1)}), bf16[16,32,3584]{2,1,0:T(8,128)(2,1)}, u32[]{:S(2)}, u32[]{:S(2)}) async-start(bf16[16,32,3584]{2,1,0:T(8,128)(2,1)} %bitcast.164), calls=%async_computation.1 | async-start | bytes 7340032 | tf_op jit(solution)/shard_map/all_to_all | solution.py:175
  71.0 2.8 %slice.176 = bf16[256,3584]{1,0:T(8,128)(2,1)} slice(bf16[256,7168]{1,0:T(8,128)(2,1)} %collective-permute-done.8.refs_10_), slice={[0:256], [3584:7168]} | slice | bytes 3670016 | tf_op jit(solution)/shard_map/slice | solution.py:288
  73.9 5.4 %reshape.447 = bf16[16,128,576]{2,1,0:T(8,128)(2,1)} reshape(bf16[16,73728]{1,0:T(8,128)(2,1)} %param.13) | data formatting | bytes 4718592 | tf_op jit(solution)/shard_map/reshape | solution.py:292
  79.3 11.0 %gather_fusion.1 = bf16[128,32,1152]{2,1,0:T(8,128)(2,1)} fusion(bf16[128,32,1152]{2,1,0:T(8,128)(2,1)} %bitcast.163, s32[1024]{0:T(1024)S(1)} %pad_clamp_fusion), kind=kCustom, calls=%fused_computation.1 | custom fusion | bytes 18874880 | tf_op jit(solution)/shard_map/gather | solution.py:291
  90.7 0.8 fusion.57
  91.9 3.6 %pad_maximum_fusion.1 = bf16[512,3584]{1,0:T(8,128)(2,1)} fusion(bf16[256,3584]{1,0:T(8,128)(2,1)} %slice.176, bf16[256,3584]{1,0:T(8,128)(2,1)S(1)} %copy-done.3), kind=kLoop, calls=%fused_computation.25 | loop fusion | flops 7340032 | bytes 7340032 | tf_op jit(solution)/shard_map/concatenate | solution.py:288
  95.5 2.0 collective-permute-done.10
  97.5 2.0 collective-permute-done.11
  99.5 1.8 pad_maximum_fusion
  101.4 0.7 copy-done.5
  102.1 1.9 fusion.22.refs_7_
  104.1 1.9 fusion.24.refs_5_
  106.1 3.4 %fusion.26.refs_8_ = f32[512,256]{1,0:T(8,128)} fusion(bf16[512,3584]{1,0:T(8,128)(2,1)S(1)} %bitcast.180, bf16[7168,256]{1,0:T(8,128)(2,1)} %collective-permute-done.7.refs_4_), kind=kOutput, calls=%fused_computation.47 | convolution fusion | flops 939524096 | bytes 6029312 | tf_op jit(solution)/shard_map/dot_general | solution.py:55
  109.5 3.4 %fusion.29.refs_6_ = f32[512,256]{1,0:T(8,128)} fusion(bf16[512,3584]{1,0:T(8,128)(2,1)S(1)} %bitcast.181, bf16[7168,256]{1,0:T(8,128)(2,1)} %collective-permute-done.6.refs_2_), kind=kOutput, calls=%fused_computation.50 | convolution fusion | flops 939524096 | bytes 6029312 | tf_op jit(solution)/shard_map/dot_general | solution.py:55
  113.6 14.0 %shard_map.131 = (bf16[512,3584]{1,0:T(8,128)(2,1)}, bf16[512,512]{1,0:T(8,128)(2,1)}) custom-call(bf16[512,3584]{1,0:T(8,128)(2,1)} %bitcast.18.refs_0_, bf16[7168,256]{1,0:T(8,128)(2,1)} %bitcast.183, bf16[7168,256]{1,0:T(8,128)(2,1)} %collective-permute-done.6.refs_2_, bf16[7168,256]{1,0:T(8,128)(2,1)} %bitcast.185, ...), custom_call_target="tpu_custom_call" | custom-call | flops 5637144576 | bytes 18350080 | tf_op jit(solution)/shard_map/pallas_call | solution.py:149
  127.7 2.5 %convolution_convert_fusion.4 = bf16[128,3584]{1,0:T(8,128)(2,1)} fusion(bf16[512,3584]{1,0:T(8,128)(2,1)S(1)} %copy-done, bf16[16,4,8,512]{3,2,1,0:T(8,128)(2,1)} %bitcast.192), kind=kOutput, calls=%fused_computation.11 | convolution fusion | flops 470220800 | bytes 4718592 | tf_op jit(solution)/shard_map/dot_general | solution.py:55
  130.2 1.6 convolution_convert_fusion.3
  132.4 0.8 collective-permute-start.12
  133.2 3.7 %collective-permute-start.13 = (bf16[128,3584]{1,0:T(8,128)(2,1)}, bf16[128,3584]{1,0:T(8,128)(2,1)}, u32[]{:S(2)}, u32[]{:S(2)}) collective-permute-start(bf16[128,3584]{1,0:T(8,128)(2,1)} %convolution_convert_fusion.3), channel_id=1, source_target_pairs={{0,4},{64,68},{4,0},{68,64},{1,5},{65,69},{5,1},{69,65},{2,6},{66,... | collective-permute-start | bytes 2752520 | tf_op jit(solution)/shard_map/ppermute | solution.py:40
  136.9 6.1 %all-to-all-start.2 = ((bf16[16,32,3584]{2,1,0:T(8,128)(2,1)}), bf16[16,32,3584]{2,1,0:T(8,128)(2,1)}, u32[]{:S(2)}, u32[]{:S(2)}) async-start(bf16[16,32,3584]{2,1,0:T(8,128)(2,1)} %bitcast.177), calls=%async_computation.2 | async-start | bytes 7340032 | tf_op jit(solution)/shard_map/all_to_all | solution.py:175
  143.1 4.3 %fusion.21 = (f32[16,128]{1,0:T(8,128)S(1)}, f32[16,128,256]{2,1,0:T(8,128)S(1)}) fusion(pred[16,256]{1,0:T(8,128)(4,1)S(1)} %get-tuple-element.83, bf16[16,256,1152]{2,1,0:T(8,128)(2,1)} %bitcast.166, bf16[16,128,576]{2,1,0:T(8,128)(2,1)S(1)} %copy-done.6), kind=kOutput, calls=%fused_computation.42 | convolution fusion | flops 672659456 | bytes 9711616 | tf_op jit(solution)/shard_map/rhc,rtc->rht/dot_general | solution.py:75
  147.5 4.5 %fusion.20 = (f32[16,128]{1,0:T(8,128)S(1)}, f32[16,128,256]{2,1,0:T(8,128)S(1)}) fusion(pred[16,256]{1,0:T(8,128)(4,1)S(1)} %get-tuple-element.84, bf16[16,256,1152]{2,1,0:T(8,128)(2,1)} %bitcast.167, bf16[16,128,576]{2,1,0:T(8,128)(2,1)S(1)} %copy-done.6), kind=kOutput, calls=%fused_computation.41 | convolution fusion | flops 672659456 | bytes 9711616 | tf_op jit(solution)/shard_map/rhc,rtc->rht/dot_general | solution.py:75
  151.9 2.2 fusion.33
  154.2 1.6 fusion.7
  155.8 2.6 %add_convert_fusion = bf16[16,128,512]{2,1,0:T(8,128)(2,1)S(1)} fusion(f32[16,128,512]{2,1,0:T(8,128)S(1)} %fusion.7, bf16[16,256,1152]{2,1,0:T(8,128)(2,1)S(1)} %bitcast.171, f32[16,128,256]{2,1,0:T(8,128)S(1)} %get-tuple-element.94, f32[16,128]{1,0:T(8,128)S(1)} %add.126, f32[16,128]{1,0:T(8,128)S(1)} %max.8, pred[16,256]{1,0:T(8,128)(4,1)S(1)} %get-tuple-element.83), kind=kOutput, calls=%fused_computation.21 | convolution fusion | flops 541589504 | bytes 12603392 | tf_op jit(solution)/shard_map/rht,rtc->rhc/dot_general | solution.py:96
  158.5 1.2 copy.60
  159.6 0.9 copy-done.1
  160.5 1.6 convolution_convert_fusion.5
  162.1 15.0 %collective-permute-done.14 = bf16[128,3584]{1,0:T(8,128)(2,1)} collective-permute-done((bf16[128,3584]{1,0:T(8,128)(2,1)S(1)}, bf16[128,3584]{1,0:T(8,128)(2,1)}, u32[]{:S(2)}, u32[]{:S(2)}) %collective-permute-start.14) | collective-permute-done | bytes 917536 | tf_op jit(solution)/shard_map/ppermute | solution.py:40
  177.2 4.2 %convolution_convert_fusion.1 = bf16[256,3584]{1,0:T(8,128)(2,1)} fusion(bf16[128,3584]{1,0:T(8,128)(2,1)} %collective-permute-done.14, bf16[128,3584]{1,0:T(8,128)(2,1)} %collective-permute-done.13, bf16[128,3584]{1,0:T(8,128)(2,1)} %collective-permute-done.12, bf16[128,3584]{1,0:T(8,128)(2,1)S(1)} %convolution_convert_fusion.5, ...), kind=kOutput, calls=%fused_computation.8 | convolution fusion | flops 956170240 | bytes 5767168 | tf_op jit(solution)/shard_map/dot_general | solution.py:55
  181.4 10.5 %all-to-all-done.2 = bf16[16,32,3584]{2,1,0:T(8,128)(2,1)} async-done(((bf16[16,32,3584]{2,1,0:T(8,128)(2,1)}), bf16[16,32,3584]{2,1,0:T(8,128)(2,1)}, u32[]{:S(2)}, u32[]{:S(2)}) %all-to-all-start.2) | async-done | bytes 3670048 | tf_op jit(solution)/shard_map/all_to_all | solution.py:175
  191.9 2.8 %convolution_convert_fusion.10 = bf16[64,3584]{1,0:T(8,128)(2,1)S(1)} fusion(bf16[64,512]{0,1:T(8,128)(2,1)S(1)} %copy-done.8, bf16[512,3584]{1,0:T(8,128)(2,1)} %bitcast.39), kind=kOutput, calls=%fused_computation.18 | convolution fusion | flops 235110400 | bytes 4194304 | tf_op jit(solution)/shard_map/dot_general | solution.py:55
  195.4 1.7 collective-permute-start.18
  197.2 1.5 collective-permute-start.19
  203.0 0.9 gather_fusion.2
  204.0 2.7 %collective-permute-start.16 = (bf16[2,65536]{1,0:T(2,128)(2,1)S(1)}, bf16[2,65536]{1,0:T(2,128)(2,1)S(1)}, u32[]{:S(2)}, u32[]{:S(2)}) collective-permute-start(bf16[2,65536]{1,0:T(2,128)(2,1)S(1)} %gather_fusion.2), channel_id=1, source_target_pairs={{0,64},{64,0},{1,65},{65,1},{2,66},{66,2},{3,67},{67,3},{4,68},{68... | collective-permute-start | bytes 786440 | tf_op jit(solution)/shard_map/ppermute | solution.py:27
  206.7 5.2 %all-to-all-start.3 = ((bf16[16,16,3584]{2,1,0:T(8,128)(2,1)}), bf16[16,16,3584]{2,1,0:T(8,128)(2,1)}, u32[]{:S(2)}, u32[]{:S(2)}) async-start(bf16[16,16,3584]{2,1,0:T(8,128)(2,1)} %bitcast.189), calls=%async_computation.3 | async-start | bytes 3670016 | tf_op jit(solution)/shard_map/all_to_all | solution.py:175
  212.5 1.1 add_convert_fusion.1
  213.6 6.9 %collective-permute-done.17 = bf16[2,65536]{1,0:T(2,128)(2,1)S(1)} collective-permute-done((bf16[2,65536]{1,0:T(2,128)(2,1)S(1)}, bf16[2,65536]{1,0:T(2,128)(2,1)S(1)}, u32[]{:S(2)}, u32[]{:S(2)}) %collective-permute-start.17) | collective-permute-done | bytes 262176 | tf_op jit(solution)/shard_map/ppermute | solution.py:27
  221.3 4.4 %dynamic_update_slice.6 = bf16[16,65536]{1,0:T(8,128)(2,1)S(1)} dynamic-update-slice(bf16[16,65536]{1,0:T(8,128)(2,1)S(1)} %bitcast.173, bf16[1,65536]{1,0:T(2,128)(2,1)S(1)} %get-tuple-element.72, s32[]{:T(128)S(6)} %select_n.233, s32[]{:T(128)} %constant.89.clone.1) | dynamic-update-slice | bytes 262148 | tf_op jit(solution)/shard_map/dynamic_update_slice | solution.py:321
  225.8 4.4 %dynamic_update_slice.7 = bf16[16,65536]{1,0:T(8,128)(2,1)S(1)} dynamic-update-slice(bf16[16,65536]{1,0:T(8,128)(2,1)S(1)} %dynamic_update_slice.6, bf16[1,65536]{1,0:T(2,128)(2,1)S(1)} %get-tuple-element.71, s32[]{:T(128)S(6)} %select_n.234, s32[]{:T(128)} %constant.89.clone.1) | dynamic-update-slice | bytes 262148 | tf_op jit(solution)/shard_map/dynamic_update_slice | solution.py:321
  230.2 9.4 %all-to-all-done.3 = bf16[16,16,3584]{2,1,0:T(8,128)(2,1)} async-done(((bf16[16,16,3584]{2,1,0:T(8,128)(2,1)}), bf16[16,16,3584]{2,1,0:T(8,128)(2,1)}, u32[]{:S(2)}, u32[]{:S(2)}) %all-to-all-start.3) | async-done | bytes 1835040 | tf_op jit(solution)/shard_map/all_to_all | solution.py:175
  239.6 1.7 reduce_sum.92
  (117 shorter events, 13.2 us)
Async XLA Ops:
  2.9 8.9 %collective-permute-start = (bf16[2,7168]{1,0:T(2,128)(2,1)S(1)}, bf16[2,7168]{1,0:T(2,128)(2,1)S(1)}, u32[]{:S(2)}, u32[]{:S(2)}) collective-permute-start(bf16[2,7168]{1,0:T(2,128)(2,1)S(1)} %gather_fusion), channel_id=1, source_target_pairs={{0,32},{32,0},{1,33},{33,1},{2,34},{34,2},{3,35},{35,3},{4,36},{36... | collective-permute-start | bytes 86024 | tf_op jit(solution)/shard_map/ppermute | solution.py:27
  3.0 9.3 %collective-permute-start.1 = (bf16[2,7168]{1,0:T(2,128)(2,1)S(1)}, bf16[2,7168]{1,0:T(2,128)(2,1)S(1)}, u32[]{:S(2)}, u32[]{:S(2)}) collective-permute-start(bf16[2,7168]{1,0:T(2,128)(2,1)S(1)} %gather_fusion), channel_id=1, source_target_pairs={{0,64},{64,0},{1,65},{65,1},{2,66},{66,2},{3,67},{67,3},{4,68},{68... | collective-permute-start | bytes 86024 | tf_op jit(solution)/shard_map/ppermute | solution.py:27
  4.3 7.9 %collective-permute-start.2 = (bf16[2,7168]{1,0:T(2,128)(2,1)S(1)}, bf16[2,7168]{1,0:T(2,128)(2,1)S(1)}, u32[]{:S(2)}, u32[]{:S(2)}) collective-permute-start(bf16[2,7168]{1,0:T(2,128)(2,1)S(1)} %gather_fusion), channel_id=1, source_target_pairs={{0,96},{32,64},{64,32},{96,0},{1,97},{33,65},{65,33},{97,1},{2,98}... | collective-permute-start | bytes 86024 | tf_op jit(solution)/shard_map/ppermute | solution.py:27
  4.8 10.8 %collective-permute-start.6 = (bf16[7168,256]{1,0:T(8,128)(2,1)}, bf16[7168,256]{1,0:T(8,128)(2,1)}, u32[]{:S(2)}, u32[]{:S(2)}) collective-permute-start(bf16[7168,256]{1,0:T(8,128)(2,1)} %bitcast.182), channel_id=1, source_target_pairs={{0,32},{32,0},{1,33},{33,1},{2,34},{34,2},{3,35},{35,3},{4,36},{36... | collective-permute-start | bytes 11010056 | tf_op jit(solution)/shard_map/ppermute | solution.py:27
  5.2 14.4 %collective-permute-start.7 = (bf16[7168,256]{1,0:T(8,128)(2,1)}, bf16[7168,256]{1,0:T(8,128)(2,1)}, u32[]{:S(2)}, u32[]{:S(2)}) collective-permute-start(bf16[7168,256]{1,0:T(8,128)(2,1)} %bitcast.184), channel_id=1, source_target_pairs={{0,32},{32,0},{1,33},{33,1},{2,34},{34,2},{3,35},{35,3},{4,36},{36... | collective-permute-start | bytes 11010056 | tf_op jit(solution)/shard_map/ppermute | solution.py:27
  7.4 12.1 %copy-start.14 = (pred[2]{0:T(512)(128)(4,1)}, pred[2]{0:T(512)(128)(4,1)S(1)}, u32[]{:S(2)}) copy-start(pred[2]{0:T(512)(128)(4,1)S(1)} %get-tuple-element.88) | copy-start | bytes 10
  11.8 30.4 %collective-permute-start.8 = (bf16[256,7168]{1,0:T(8,128)(2,1)}, bf16[256,7168]{1,0:T(8,128)(2,1)}, u32[]{:S(2)}, u32[]{:S(2)}) collective-permute-start(bf16[256,7168]{1,0:T(8,128)(2,1)} %bitcast.174), channel_id=1, source_target_pairs={{0,32},{32,0},{1,33},{33,1},{2,34},{34,2},{3,35},{35,3},{4,36},{36... | collective-permute-start | bytes 11010056 | tf_op jit(solution)/shard_map/ppermute | solution.py:27
  13.7 15.2 %collective-permute-start.3 = (bf16[16,3712]{1,0:T(8,128)(2,1)S(1)}, bf16[16,3712]{1,0:T(8,128)(2,1)S(1)}, u32[]{:S(2)}, u32[]{:S(2)}) collective-permute-start(bf16[16,3712]{1,0:T(8,128)(2,1)S(1)} %concatenate.22), channel_id=1, source_target_pairs={{0,64},{64,4},{4,68},{68,0},{1,65},{65,5},{5,69},{69,1},{2,66},{66... | collective-permute-start | bytes 356360 | tf_op jit(solution)/shard_map/ppermute | solution.py:40
  15.0 14.0 %collective-permute-start.4 = (bf16[16,3712]{1,0:T(8,128)(2,1)S(1)}, bf16[16,3712]{1,0:T(8,128)(2,1)S(1)}, u32[]{:S(2)}, u32[]{:S(2)}) collective-permute-start(bf16[16,3712]{1,0:T(8,128)(2,1)S(1)} %concatenate.22), channel_id=1, source_target_pairs={{0,4},{64,68},{4,0},{68,64},{1,5},{65,69},{5,1},{69,65},{2,6},{66,... | collective-permute-start | bytes 356360 | tf_op jit(solution)/shard_map/ppermute | solution.py:40
  15.6 13.3 %collective-permute-start.5 = (bf16[16,3712]{1,0:T(8,128)(2,1)S(1)}, bf16[16,3712]{1,0:T(8,128)(2,1)S(1)}, u32[]{:S(2)}, u32[]{:S(2)}) collective-permute-start(bf16[16,3712]{1,0:T(8,128)(2,1)S(1)} %concatenate.22), channel_id=1, source_target_pairs={{0,68},{64,0},{4,64},{68,4},{1,69},{65,1},{5,65},{69,5},{2,70},{66... | collective-permute-start | bytes 356360 | tf_op jit(solution)/shard_map/ppermute | solution.py:40
  21.0 35.1 %all-to-all-start = ((bf16[16,16,3712]{2,1,0:T(8,128)(2,1)}), bf16[16,16,3712]{2,1,0:T(8,128)(2,1)S(1)}, u32[]{:S(2)}, u32[]{:S(2)}) async-start(bf16[16,16,3712]{2,1,0:T(8,128)(2,1)} %broadcast_in_dim.148), calls=%async_computation | async-start | bytes 3801088 | tf_op jit(solution)/shard_map/all_to_all | solution.py:175
  57.9 37.6 %collective-permute-start.9 = (bf16[128,3584]{1,0:T(8,128)(2,1)}, bf16[128,3584]{1,0:T(8,128)(2,1)S(1)}, u32[]{:S(2)}, u32[]{:S(2)}) collective-permute-start(bf16[128,3584]{1,0:T(8,128)(2,1)} %convolution_convert_fusion.8), channel_id=1, source_target_pairs={{0,64},{64,4},{4,68},{68,0},{1,65},{65,5},{5,69},{69,1},{2,66},{66... | collective-permute-start | bytes 2752520 | tf_op jit(solution)/shard_map/ppermute | solution.py:40
  60.7 36.8 %collective-permute-start.10 = (bf16[128,3584]{1,0:T(8,128)(2,1)}, bf16[128,3584]{1,0:T(8,128)(2,1)}, u32[]{:S(2)}, u32[]{:S(2)}) collective-permute-start(bf16[128,3584]{1,0:T(8,128)(2,1)} %convolution_convert_fusion.7), channel_id=1, source_target_pairs={{0,4},{64,68},{4,0},{68,64},{1,5},{65,69},{5,1},{69,65},{2,6},{66,... | collective-permute-start | bytes 2752520 | tf_op jit(solution)/shard_map/ppermute | solution.py:40
  64.3 35.2 %collective-permute-start.11 = (bf16[128,3584]{1,0:T(8,128)(2,1)}, bf16[128,3584]{1,0:T(8,128)(2,1)}, u32[]{:S(2)}, u32[]{:S(2)}) collective-permute-start(bf16[128,3584]{1,0:T(8,128)(2,1)} %convolution_convert_fusion.6), channel_id=1, source_target_pairs={{0,68},{64,0},{4,64},{68,4},{1,69},{65,1},{5,65},{69,5},{2,70},{66... | collective-permute-start | bytes 2752520 | tf_op jit(solution)/shard_map/ppermute | solution.py:40
  66.3 47.3 %all-to-all-start.1 = ((bf16[16,32,3584]{2,1,0:T(8,128)(2,1)}), bf16[16,32,3584]{2,1,0:T(8,128)(2,1)}, u32[]{:S(2)}, u32[]{:S(2)}) async-start(bf16[16,32,3584]{2,1,0:T(8,128)(2,1)} %bitcast.164), calls=%async_computation.1 | async-start | bytes 7340032 | tf_op jit(solution)/shard_map/all_to_all | solution.py:175
  90.3 1.6 copy-start.3
  99.5 2.6 %copy-start.5 = (bf16[1,7168,256]{2,1,0:T(8,128)(2,1)S(1)}, bf16[1,7168,256]{2,1,0:T(8,128)(2,1)}, u32[]{:S(2)}) copy-start(bf16[1,7168,256]{2,1,0:T(8,128)(2,1)} %param.22) | copy-start | bytes 11010052
  102.1 2.0 copy-start.4
  113.6 14.0 %copy-start = (bf16[512,3584]{1,0:T(8,128)(2,1)S(1)}, bf16[512,3584]{1,0:T(8,128)(2,1)}, u32[]{:S(2)}) copy-start(bf16[512,3584]{1,0:T(8,128)(2,1)} %pad_maximum_fusion.1) | copy-start | bytes 11010052
  127.6 2.6 %copy-start.7 = (bf16[512,512]{1,0:T(8,128)(2,1)S(1)}, bf16[512,512]{1,0:T(8,128)(2,1)}, u32[]{:S(2)}) copy-start(bf16[512,512]{1,0:T(8,128)(2,1)} %get-tuple-element.49) | copy-start | bytes 1572868
  132.4 29.7 %collective-permute-start.12 = (bf16[128,3584]{1,0:T(8,128)(2,1)}, bf16[128,3584]{1,0:T(8,128)(2,1)}, u32[]{:S(2)}, u32[]{:S(2)}) collective-permute-start(bf16[128,3584]{1,0:T(8,128)(2,1)} %convolution_convert_fusion.4), channel_id=1, source_target_pairs={{0,68},{64,0},{4,64},{68,4},{1,69},{65,1},{5,65},{69,5},{2,70},{66... | collective-permute-start | bytes 2752520 | tf_op jit(solution)/shard_map/ppermute | solution.py:40
  133.2 28.9 %collective-permute-start.13 = (bf16[128,3584]{1,0:T(8,128)(2,1)}, bf16[128,3584]{1,0:T(8,128)(2,1)}, u32[]{:S(2)}, u32[]{:S(2)}) collective-permute-start(bf16[128,3584]{1,0:T(8,128)(2,1)} %convolution_convert_fusion.3), channel_id=1, source_target_pairs={{0,4},{64,68},{4,0},{68,64},{1,5},{65,69},{5,1},{69,65},{2,6},{66,... | collective-permute-start | bytes 2752520 | tf_op jit(solution)/shard_map/ppermute | solution.py:40
  136.9 40.2 %collective-permute-start.14 = (bf16[128,3584]{1,0:T(8,128)(2,1)S(1)}, bf16[128,3584]{1,0:T(8,128)(2,1)}, u32[]{:S(2)}, u32[]{:S(2)}) collective-permute-start(bf16[128,3584]{1,0:T(8,128)(2,1)S(1)} %convolution_convert_fusion.2), channel_id=1, source_target_pairs={{0,64},{64,4},{4,68},{68,0},{1,65},{65,5},{5,69},{69,1},{2,66},{66... | collective-permute-start | bytes 2752520 | tf_op jit(solution)/shard_map/ppermute | solution.py:40
  136.9 6.1 %copy-start.6 = (bf16[16,128,576]{2,1,0:T(8,128)(2,1)S(1)}, bf16[16,128,576]{2,1,0:T(8,128)(2,1)}, u32[]{:S(2)}) copy-start(bf16[16,128,576]{2,1,0:T(8,128)(2,1)} %reshape.447) | copy-start | bytes 7077892
  136.9 55.0 %all-to-all-start.2 = ((bf16[16,32,3584]{2,1,0:T(8,128)(2,1)}), bf16[16,32,3584]{2,1,0:T(8,128)(2,1)}, u32[]{:S(2)}, u32[]{:S(2)}) async-start(bf16[16,32,3584]{2,1,0:T(8,128)(2,1)} %bitcast.177), calls=%async_computation.2 | async-start | bytes 7340032 | tf_op jit(solution)/shard_map/all_to_all | solution.py:175
  143.1 11.1 %slice-start = ((s8[9437184]{0:T(1024)(128)(4,1)}), s8[4194304]{0:T(1024)(128)(4,1)S(1)}, s32[]{:S(2)}) async-start(s8[9437184]{0:T(1024)(128)(4,1)} %bitcast.168), calls=%async_computation.4 | async-start | bytes 8388608
  143.1 11.1 %slice-start.1 = ((s8[9437184]{0:T(1024)(128)(4,1)}), s8[4194304]{0:T(1024)(128)(4,1)S(1)}, s32[]{:S(2)}) async-start(s8[9437184]{0:T(1024)(128)(4,1)} %bitcast.168), calls=%async_computation.5 | async-start | bytes 8388608
  147.4 6.7 %slice-start.2 = ((s8[9437184]{0:T(1024)(128)(4,1)}), s8[1048576]{0:T(1024)(128)(4,1)S(1)}, s32[]{:S(2)}) async-start(s8[9437184]{0:T(1024)(128)(4,1)} %bitcast.168), calls=%async_computation.6 | async-start | bytes 2097152
  158.5 2.0 copy-start.1
  160.5 16.7 %copy-start.10 = (bf16[256,128]{0,1:T(8,128)(2,1)S(1)}, bf16[256,128]{0,1:T(8,128)(2,1)}, u32[]{:S(2)}) copy-start(bf16[256,128]{0,1:T(8,128)(2,1)} %get-tuple-element.79) | copy-start | bytes 196612
  160.5 16.7 %copy-start.11 = (bf16[256,128]{0,1:T(8,128)(2,1)S(1)}, bf16[256,128]{0,1:T(8,128)(2,1)}, u32[]{:S(2)}) copy-start(bf16[256,128]{0,1:T(8,128)(2,1)} %get-tuple-element.80) | copy-start | bytes 196612
  160.5 16.7 %copy-start.12 = (bf16[256,128]{0,1:T(8,128)(2,1)S(1)}, bf16[256,128]{0,1:T(8,128)(2,1)}, u32[]{:S(2)}) copy-start(bf16[256,128]{0,1:T(8,128)(2,1)} %get-tuple-element.81) | copy-start | bytes 196612
  160.5 16.7 %copy-start.13 = (bf16[256,128]{0,1:T(8,128)(2,1)S(1)}, bf16[256,128]{0,1:T(8,128)(2,1)}, u32[]{:S(2)}) copy-start(bf16[256,128]{0,1:T(8,128)(2,1)} %get-tuple-element.82) | copy-start | bytes 196612
  177.2 14.7 %copy-start.8 = (bf16[64,512]{0,1:T(8,128)(2,1)S(1)}, bf16[64,512]{0,1:T(8,128)(2,1)}, u32[]{:S(2)}) copy-start(bf16[64,512]{0,1:T(8,128)(2,1)} %fusion.56) | copy-start | bytes 196612
  195.4 16.4 %collective-permute-start.18 = (bf16[16,3584]{1,0:T(8,128)(2,1)}, bf16[16,3584]{1,0:T(8,128)(2,1)S(1)}, u32[]{:S(2)}, u32[]{:S(2)}) collective-permute-start(bf16[16,3584]{1,0:T(8,128)(2,1)} %get-tuple-element.68), channel_id=1, source_target_pairs={{0,68},{64,0},{4,64},{68,4},{1,69},{65,1},{5,65},{69,5},{2,70},{66... | collective-permute-start | bytes 344072 | tf_op jit(solution)/shard_map/ppermute | solution.py:40
  197.2 14.8 %collective-permute-start.19 = (bf16[16,3584]{1,0:T(8,128)(2,1)}, bf16[16,3584]{1,0:T(8,128)(2,1)}, u32[]{:S(2)}, u32[]{:S(2)}) collective-permute-start(bf16[16,3584]{1,0:T(8,128)(2,1)} %get-tuple-element.70), channel_id=1, source_target_pairs={{0,4},{64,68},{4,0},{68,64},{1,5},{65,69},{5,1},{69,65},{2,6},{66,... | collective-permute-start | bytes 344072 | tf_op jit(solution)/shard_map/ppermute | solution.py:40
  198.7 13.8 %collective-permute-start.20 = (bf16[16,3584]{1,0:T(8,128)(2,1)}, bf16[16,3584]{1,0:T(8,128)(2,1)}, u32[]{:S(2)}, u32[]{:S(2)}) collective-permute-start(bf16[16,3584]{1,0:T(8,128)(2,1)} %get-tuple-element.69), channel_id=1, source_target_pairs={{0,64},{64,4},{4,68},{68,0},{1,65},{65,5},{5,69},{69,1},{2,66},{66... | collective-permute-start | bytes 344072 | tf_op jit(solution)/shard_map/ppermute | solution.py:40
  203.9 16.6 %copy-start.15 = (pred[2]{0:T(512)(128)(4,1)S(1)}, pred[2]{0:T(512)(128)(4,1)}, u32[]{:S(2)}) copy-start(pred[2]{0:T(512)(128)(4,1)} %copy-done.14) | copy-start | bytes 10
  203.9 9.7 %collective-permute-start.15 = (bf16[2,65536]{1,0:T(2,128)(2,1)S(1)}, bf16[2,65536]{1,0:T(2,128)(2,1)S(1)}, u32[]{:S(2)}, u32[]{:S(2)}) collective-permute-start(bf16[2,65536]{1,0:T(2,128)(2,1)S(1)} %gather_fusion.2), channel_id=1, source_target_pairs={{0,32},{32,0},{1,33},{33,1},{2,34},{34,2},{3,35},{35,3},{4,36},{36... | collective-permute-start | bytes 786440 | tf_op jit(solution)/shard_map/ppermute | solution.py:27
  204.0 9.6 %collective-permute-start.16 = (bf16[2,65536]{1,0:T(2,128)(2,1)S(1)}, bf16[2,65536]{1,0:T(2,128)(2,1)S(1)}, u32[]{:S(2)}, u32[]{:S(2)}) collective-permute-start(bf16[2,65536]{1,0:T(2,128)(2,1)S(1)} %gather_fusion.2), channel_id=1, source_target_pairs={{0,64},{64,0},{1,65},{65,1},{2,66},{66,2},{3,67},{67,3},{4,68},{68... | collective-permute-start | bytes 786440 | tf_op jit(solution)/shard_map/ppermute | solution.py:27
  206.7 32.9 %all-to-all-start.3 = ((bf16[16,16,3584]{2,1,0:T(8,128)(2,1)}), bf16[16,16,3584]{2,1,0:T(8,128)(2,1)}, u32[]{:S(2)}, u32[]{:S(2)}) async-start(bf16[16,16,3584]{2,1,0:T(8,128)(2,1)} %bitcast.189), calls=%async_computation.3 | async-start | bytes 3670016 | tf_op jit(solution)/shard_map/all_to_all | solution.py:175
  211.9 0.6 copy-start.9
  211.9 8.6 %collective-permute-start.17 = (bf16[2,65536]{1,0:T(2,128)(2,1)S(1)}, bf16[2,65536]{1,0:T(2,128)(2,1)S(1)}, u32[]{:S(2)}, u32[]{:S(2)}) collective-permute-start(bf16[2,65536]{1,0:T(2,128)(2,1)S(1)} %gather_fusion.2), channel_id=1, source_target_pairs={{0,96},{32,64},{64,32},{96,0},{1,97},{33,65},{65,33},{97,1},{2,98}... | collective-permute-start | bytes 786440 | tf_op jit(solution)/shard_map/ppermute | solution.py:27
  230.2 11.8 %copy-start.2 = (bf16[16,65536]{1,0:T(8,128)(2,1)}, bf16[16,65536]{1,0:T(8,128)(2,1)S(1)}, u32[]{:S(2)}) copy-start(bf16[16,65536]{1,0:T(8,128)(2,1)S(1)} %dynamic_update_slice.7) | copy-start | bytes 6291460
